TPU v7x, 32 devices: a whole 2x2x4 slice. The times are simulated.
32 devices in a mesh: dp: 8 (over z, y), expert: 4 (over x, core).
Axes of the slice: x: 2, y: 2, z: 4, core: 2. Of those that a mesh axis runs over, the one named last changes fastest.
Arguments:
- model_predictions: bfloat16 [4, 4096, 4416], P('expert', 'dp'), may hold values from -18 to 18
- member_tile_presence: int32 [4, 4096], P('expert', 'dp'), may hold values 0 or 1
- piece_usable_flags: int32 [4096], P(('dp', 'expert')), may hold values from 0 to 1, as said below
- horizon_positions: int32 [8], P('dp'), may hold values from 0 to 7, as said below
- result_adjoint: bfloat16 [4096, 4416], P(('dp', 'expert')), may hold values from -6 to 6
- tile_lift_matrix: bfloat16 [4416, 768], replicated, may hold values from -0.09375 to 0.09375
- tile_lift_offset: bfloat16 [768], replicated, may hold values from -3 to 3
- horizon_lookup: bfloat16 [8, 768], replicated, may hold values from -3 to 3
- normalizer_scales: bfloat16 [3, 768], replicated, may hold values from 0.5 to 1.5
- normalizer_offsets: bfloat16 [3, 768], replicated, may hold values from -1.25 to 1.25
- query_key_value_matrix: bfloat16 [768, 2304], replicated, may hold values from -0.21875 to 0.21875
- attend_result_matrix: bfloat16 [768, 768], replicated, may hold values from -3 to 3
- attend_offset_vector: bfloat16 [768], replicated, may hold values from -1.75 to 1.75
- expand_matrix: bfloat16 [768, 3072], replicated, may hold values from -0.21875 to 0.21875
- expand_offset: bfloat16 [3072], replicated, may hold values from -1.75 to 1.75
- contract_matrix: bfloat16 [3072, 768], replicated, may hold values from -0.21875 to 0.21875
- contract_offset: bfloat16 [768], replicated, may hold values from -1.75 to 1.75
- mixing_head_matrix: bfloat16 [768, 276], replicated, may hold values from -0.15625 to 0.15625
- mixing_head_offset: bfloat16 [276], replicated, may hold values from -0.625 to 0.625
Outputs:
- combined_prediction: bfloat16 [4096, 4416], P(('dp', 'expert'))
- model_predictions_slope: bfloat16 [4, 4096, 4416], P('expert', 'dp')
- sublevel_magnitudes: float32 [4], replicated
- tile_lift_matrix_slope: float32 [4416, 768], P('dp')
- tile_lift_offset_slope: float32 [768], replicated
- horizon_lookup_slope: float32 [8, 768], replicated
- normalizer_scales_slope: float32 [3, 768], replicated
- normalizer_offsets_slope: float32 [3, 768], replicated
- query_key_value_slope: float32 [768, 2304], P('dp')
- attend_result_slope: float32 [768, 768], P('dp')
- attend_offset_slope: float32 [768], replicated
- expand_matrix_slope: float32 [768, 3072], P('dp')
- expand_offset_slope: float32 [3072], replicated
- contract_matrix_slope: float32 [3072, 768], P('dp')
- contract_offset_slope: float32 [768], replicated
- mixing_head_matrix_slope: float32 [768, 276], P('dp')
- mixing_head_offset_slope: float32 [276], replicated
Inputs may be any that keep to these rules, and one draw needn't show every extreme that they name: `piece_usable_flags`: the first patch of every frame is valid. `horizon_positions`: some frame has lead 0 and some frame has lead 8 - 1.
All inputs are finite; a program needn't handle non-finite values. No bound on the sum of `member_tile_presence` on one device may be relied on, other than what follows from the above.
Results may differ from a plain program's by a relative error of at most 0.015.
Values may be sent and summed in bfloat16 or wider, within the bound.
No kernel may reach another device: no remote copies, remote signals or barrier semaphores. Data moves between devices by JAX's collectives and lax.ppermute only.
A program may use at most 192 MiB of HBM per device.

v0:
```python
import jax
import jax.numpy as jnp
from jax import lax
from jax.sharding import PartitionSpec as P

D = 768
HEADS = 12
HEAD_DIM = 64
MODEL_TALLY = 3
CHANNELS = 69
PIXELS = 64
TILE_ENTRIES = 4416


NORM_EPSILON = 1e-05
SQUARE_EPSILON = 1e-06
MASKED_SCORE = -1e30


def normalize(values, gain_row, offset_row):
    center = values - jnp.mean(values, axis=-1, keepdims=True)
    inverse = lax.rsqrt(jnp.mean(center * center, axis=-1, keepdims=True) + NORM_EPSILON)
    unit_rows = center * inverse
    return (unit_rows * gain_row + offset_row, unit_rows, inverse)


def normalize_back(grad_out, unit_rows, inverse, gain_row):
    scaled = grad_out * gain_row
    grad_in = inverse * (
        scaled
        - jnp.mean(scaled, axis=-1, keepdims=True)
        - unit_rows * jnp.mean(scaled * unit_rows, axis=-1, keepdims=True)
    )
    return (grad_in, jnp.sum(grad_out * unit_rows, axis=0), jnp.sum(grad_out, axis=0))


def interior_lines(former, latter):
    return lax.dot_general(
        former, latter, (((0,), (0,)), ((), ())), preferred_element_type=jnp.float32
    )


def product_flipped(former, latter):
    return lax.dot_general(
        former, latter, (((1,), (1,)), ((), ())), preferred_element_type=jnp.float32
    )


def square_sum(values, valid_rows):
    return jnp.sum(jnp.sum(values * values, axis=-1) * valid_rows)


def masked_scores(queries, keys_all, key_flags):
    raw_scores = jnp.einsum("qhd,khd->hqk", queries, keys_all, preferred_element_type=jnp.float32)
    return jnp.where(key_flags[None, None, :] > 0, raw_scores * HEAD_DIM ** (-0.5), MASKED_SCORE)


def local(
    model_predictions,
    member_tile_presence,
    piece_usable_flags,
    horizon_positions,
    result_adjoint,
    tile_lift_matrix,
    tile_lift_offset,
    horizon_lookup,
    normalizer_scales,
    normalizer_offsets,
    query_key_value_matrix,
    attend_result_matrix,
    attend_offset_vector,
    expand_matrix,
    expand_offset,
    contract_matrix,
    contract_offset,
    mixing_head_matrix,
    mixing_head_offset,
):
    expert_slots = lax.axis_size("expert")
    active = (lax.axis_index("expert") < MODEL_TALLY).astype(jnp.float32)
    device_prediction = model_predictions[0]
    own_mask = member_tile_presence[0].astype(jnp.float32) * active
    local_embed = (
        jnp.dot(device_prediction, tile_lift_matrix, preferred_element_type=jnp.float32)
        * own_mask[:, None]
    )
    all_predictions = lax.all_to_all(
        model_predictions, "expert", split_axis=1, concat_axis=0, tiled=True
    )
    embedded = lax.psum_scatter(local_embed, "expert", scatter_dimension=0, tiled=True)
    row_count = embedded.shape[0]
    gain_rows = normalizer_scales.astype(jnp.float32)
    shift_rows = normalizer_offsets.astype(jnp.float32)
    valid_rows = piece_usable_flags.astype(jnp.float32)
    stream_in = embedded + tile_lift_offset.astype(jnp.float32)
    lead_hot = (jnp.arange(horizon_lookup.shape[0]) == horizon_positions[0]).astype(jnp.bfloat16)
    lead_vector = jnp.dot(lead_hot, horizon_lookup, preferred_element_type=jnp.float32)
    normed, unit_one, inverse_one = normalize(stream_in, gain_rows[0], shift_rows[0])
    normed_one = (normed + lead_vector).astype(jnp.bfloat16)
    triple = jnp.dot(normed_one, query_key_value_matrix, preferred_element_type=jnp.float32).astype(
        jnp.bfloat16
    )
    queries = triple[:, :D].reshape(row_count, HEADS, HEAD_DIM)
    keys_flat, values_flat, key_flags = (
        lax.all_gather(triple[:, D : 2 * D], "expert", axis=0, tiled=True),
        lax.all_gather(triple[:, 2 * D :], "expert", axis=0, tiled=True),
        lax.all_gather(piece_usable_flags.astype(jnp.bfloat16), "expert", axis=0, tiled=True),
    )
    key_count = keys_flat.shape[0]
    keys_all = keys_flat.reshape(key_count, HEADS, HEAD_DIM)
    values_all = values_flat.reshape(key_count, HEADS, HEAD_DIM)
    scores = masked_scores(queries, keys_all, key_flags)
    maxima = jnp.max(scores, axis=-1, keepdims=True)
    log_norm = maxima + jnp.log(jnp.sum(jnp.exp(scores - maxima), axis=-1, keepdims=True))
    chance_low = jnp.exp(scores - log_norm).astype(jnp.bfloat16)
    mixed = jnp.einsum("hqk,khd->qhd", chance_low, values_all, preferred_element_type=jnp.float32)
    mixed = mixed.astype(jnp.bfloat16).reshape(row_count, D)
    attend_out = jnp.dot(
        mixed, attend_result_matrix, preferred_element_type=jnp.float32
    ) + attend_offset_vector.astype(jnp.float32)
    stream_mid = stream_in + attend_out
    normed, unit_two, inverse_two = normalize(stream_mid, gain_rows[1], shift_rows[1])
    normed_two = normed.astype(jnp.bfloat16)
    hidden = jnp.dot(
        normed_two, expand_matrix, preferred_element_type=jnp.float32
    ) + expand_offset.astype(jnp.float32)
    activated = jax.nn.gelu(hidden).astype(jnp.bfloat16)
    feed_out = jnp.dot(
        activated, contract_matrix, preferred_element_type=jnp.float32
    ) + contract_offset.astype(jnp.float32)
    stream_out = stream_mid + feed_out
    normed, unit_three, inverse_three = normalize(stream_out, gain_rows[2], shift_rows[2])
    normed_three = normed.astype(jnp.bfloat16)
    head_vals = jnp.dot(
        normed_three, mixing_head_matrix, preferred_element_type=jnp.float32
    ) + mixing_head_offset.astype(jnp.float32)
    logits = head_vals[:, : MODEL_TALLY * CHANNELS].reshape(row_count, MODEL_TALLY, CHANNELS)
    shift_out = head_vals[:, MODEL_TALLY * CHANNELS :]
    logit_top = jnp.max(logits, axis=1, keepdims=True)
    powers = jnp.exp(logits - logit_top)
    blend_weights = powers / jnp.sum(powers, axis=1, keepdims=True)
    present_prediction = all_predictions[:MODEL_TALLY].astype(jnp.float32)
    wide_weights = jnp.repeat(jnp.transpose(blend_weights, (1, 0, 2)), PIXELS, axis=2)
    combined_prediction = jnp.sum(wide_weights * present_prediction, axis=0) + jnp.repeat(
        shift_out, PIXELS, axis=1
    )
    stat_local = jnp.stack(
        [
            square_sum(stream_in, valid_rows),
            square_sum(attend_out, valid_rows),
            square_sum(feed_out, valid_rows),
            square_sum(stream_out, valid_rows),
            jnp.sum(valid_rows),
        ]
    )
    stat_total = lax.psum(stat_local, ("dp", "expert"))
    grad_blend = result_adjoint.astype(jnp.float32)
    fore_back = wide_weights * grad_blend[None]
    spare_slots = jnp.zeros((expert_slots - MODEL_TALLY, row_count, TILE_ENTRIES), jnp.float32)
    returned = lax.all_to_all(
        jnp.concatenate([fore_back, spare_slots], axis=0).astype(jnp.bfloat16),
        "expert",
        split_axis=0,
        concat_axis=1,
        tiled=True,
    ).astype(jnp.float32)
    mixture_share = returned[0]
    products = (present_prediction * grad_blend[None]).reshape(
        MODEL_TALLY, row_count, CHANNELS, PIXELS
    )
    grad_weights = jnp.transpose(jnp.sum(products, axis=-1), (1, 0, 2))
    grad_shift = jnp.sum(grad_blend.reshape(row_count, CHANNELS, PIXELS), axis=-1)
    grad_logits = blend_weights * (
        grad_weights - jnp.sum(blend_weights * grad_weights, axis=1, keepdims=True)
    )
    grad_head_vals = jnp.concatenate(
        [grad_logits.reshape(row_count, MODEL_TALLY * CHANNELS), grad_shift], axis=1
    )
    bias_head_grad = jnp.sum(grad_head_vals, axis=0)
    head_low = grad_head_vals.astype(jnp.bfloat16)
    weight_head_grad = interior_lines(normed_three, head_low)
    grad_normed_three = product_flipped(head_low, mixing_head_matrix)
    grad_stream_out, gain_three, shift_three = normalize_back(
        grad_normed_three, unit_three, inverse_three, gain_rows[2]
    )
    bias_reduce_grad = jnp.sum(grad_stream_out, axis=0)
    feed_low = grad_stream_out.astype(jnp.bfloat16)
    weight_reduce_grad = interior_lines(activated, feed_low)
    grad_activated = product_flipped(feed_low, contract_matrix)
    _, gelu_back = jax.vjp(jax.nn.gelu, hidden)
    grad_hidden = gelu_back(grad_activated)[0]
    bias_expand_grad = jnp.sum(grad_hidden, axis=0)
    hidden_low = grad_hidden.astype(jnp.bfloat16)
    weight_expand_grad = interior_lines(normed_two, hidden_low)
    grad_normed_two = product_flipped(hidden_low, expand_matrix)
    grad_mid_norm, gain_two, shift_two = normalize_back(
        grad_normed_two, unit_two, inverse_two, gain_rows[1]
    )
    grad_stream_mid = grad_stream_out + grad_mid_norm
    bias_heads_grad = jnp.sum(grad_stream_mid, axis=0)
    attend_low = grad_stream_mid.astype(jnp.bfloat16)
    weight_out_grad = interior_lines(mixed, attend_low)
    grad_mixed = (
        product_flipped(attend_low, attend_result_matrix)
        .astype(jnp.bfloat16)
        .reshape(row_count, HEADS, HEAD_DIM)
    )
    scores = masked_scores(queries, keys_all, key_flags)
    chance = jnp.exp(scores - log_norm)
    value_part = jnp.einsum(
        "hqk,qhd->khd", chance.astype(jnp.bfloat16), grad_mixed, preferred_element_type=jnp.float32
    )
    grad_chance = jnp.einsum(
        "qhd,khd->hqk", grad_mixed, values_all, preferred_element_type=jnp.float32
    )
    delta_rows = jnp.sum(chance * grad_chance, axis=-1, keepdims=True)
    grad_scores = (chance * (grad_chance - delta_rows) * HEAD_DIM ** (-0.5)).astype(jnp.bfloat16)
    grad_queries = jnp.einsum(
        "hqk,khd->qhd", grad_scores, keys_all, preferred_element_type=jnp.float32
    )
    key_part = jnp.einsum("hqk,qhd->khd", grad_scores, queries, preferred_element_type=jnp.float32)
    grad_keys, grad_values = (
        lax.psum_scatter(
            key_part.reshape(key_count, D).astype(jnp.bfloat16),
            "expert",
            scatter_dimension=0,
            tiled=True,
        ).astype(jnp.float32),
        lax.psum_scatter(
            value_part.reshape(key_count, D).astype(jnp.bfloat16),
            "expert",
            scatter_dimension=0,
            tiled=True,
        ).astype(jnp.float32),
    )
    grad_triple = jnp.concatenate(
        [grad_queries.reshape(row_count, D), grad_keys, grad_values], axis=1
    )
    triple_low = grad_triple.astype(jnp.bfloat16)
    weight_in_grad = interior_lines(normed_one, triple_low)
    grad_normed_one = product_flipped(triple_low, query_key_value_matrix)
    lead_grad = lead_hot.astype(jnp.float32)[:, None] * jnp.sum(grad_normed_one, axis=0)[None, :]
    grad_in_norm, gain_one, shift_one = normalize_back(
        grad_normed_one, unit_one, inverse_one, gain_rows[0]
    )
    grad_stream_in = grad_stream_mid + grad_in_norm
    bias_embed_grad = jnp.sum(grad_stream_in, axis=0)
    embed_low = grad_stream_in.astype(jnp.bfloat16)
    whole_grad = lax.all_gather(embed_low, "expert", axis=0, tiled=True)
    screened_derivative = whole_grad * own_mask.astype(jnp.bfloat16)[:, None]
    lift_matrix_derivative = interior_lines(device_prediction, screened_derivative)
    prediction_slope = product_flipped(screened_derivative, tile_lift_matrix) + mixture_share
    model_predictions_slope = prediction_slope.astype(jnp.bfloat16)[None]
    gain_grads = jnp.stack([gain_one, gain_two, gain_three])
    shift_grads = jnp.stack([shift_one, shift_two, shift_three])
    row_shares = (
        lax.psum_scatter(lift_matrix_derivative, "dp", scatter_dimension=0, tiled=True),
        lax.psum_scatter(weight_in_grad, "dp", scatter_dimension=0, tiled=True),
        lax.psum_scatter(weight_out_grad, "dp", scatter_dimension=0, tiled=True),
        lax.psum_scatter(weight_expand_grad, "dp", scatter_dimension=0, tiled=True),
        lax.psum_scatter(weight_reduce_grad, "dp", scatter_dimension=0, tiled=True),
        lax.psum_scatter(weight_head_grad, "dp", scatter_dimension=0, tiled=True),
    )
    column_shares = (
        lax.psum_scatter(
            row_shares[0].astype(jnp.bfloat16), "expert", scatter_dimension=1, tiled=True
        ).astype(jnp.float32),
        lax.psum_scatter(
            row_shares[1].astype(jnp.bfloat16), "expert", scatter_dimension=1, tiled=True
        ).astype(jnp.float32),
        lax.psum_scatter(
            row_shares[2].astype(jnp.bfloat16), "expert", scatter_dimension=1, tiled=True
        ).astype(jnp.float32),
        lax.psum_scatter(
            row_shares[3].astype(jnp.bfloat16), "expert", scatter_dimension=1, tiled=True
        ).astype(jnp.float32),
        lax.psum_scatter(
            row_shares[4].astype(jnp.bfloat16), "expert", scatter_dimension=1, tiled=True
        ).astype(jnp.float32),
        lax.psum_scatter(
            row_shares[5].astype(jnp.bfloat16), "expert", scatter_dimension=1, tiled=True
        ).astype(jnp.float32),
    )
    (
        tile_lift_matrix_slope,
        query_key_value_slope,
        attend_result_slope,
        expand_matrix_slope,
        contract_matrix_slope,
        mixing_head_matrix_slope,
    ) = (
        lax.all_gather(column_shares[0].astype(jnp.bfloat16), "expert", axis=1, tiled=True).astype(
            jnp.float32
        ),
        lax.all_gather(column_shares[1].astype(jnp.bfloat16), "expert", axis=1, tiled=True).astype(
            jnp.float32
        ),
        lax.all_gather(column_shares[2].astype(jnp.bfloat16), "expert", axis=1, tiled=True).astype(
            jnp.float32
        ),
        lax.all_gather(column_shares[3].astype(jnp.bfloat16), "expert", axis=1, tiled=True).astype(
            jnp.float32
        ),
        lax.all_gather(column_shares[4].astype(jnp.bfloat16), "expert", axis=1, tiled=True).astype(
            jnp.float32
        ),
        lax.all_gather(column_shares[5].astype(jnp.bfloat16), "expert", axis=1, tiled=True).astype(
            jnp.float32
        ),
    )
    (
        tile_lift_offset_slope,
        horizon_lookup_slope,
        normalizer_scales_slope,
        normalizer_offsets_slope,
        attend_offset_slope,
        expand_offset_slope,
        contract_offset_slope,
        mixing_head_offset_slope,
    ) = lax.psum(
        (
            bias_embed_grad,
            lead_grad,
            gain_grads,
            shift_grads,
            bias_heads_grad,
            bias_expand_grad,
            bias_reduce_grad,
            bias_head_grad,
        ),
        ("dp", "expert"),
    )
    sublevel_magnitudes = jnp.sqrt(stat_total[:4] / (stat_total[4] * D) + SQUARE_EPSILON)
    return (
        combined_prediction.astype(jnp.bfloat16),
        model_predictions_slope,
        sublevel_magnitudes,
        tile_lift_matrix_slope,
        tile_lift_offset_slope,
        horizon_lookup_slope,
        normalizer_scales_slope,
        normalizer_offsets_slope,
        query_key_value_slope,
        attend_result_slope,
        attend_offset_slope,
        expand_matrix_slope,
        expand_offset_slope,
        contract_matrix_slope,
        contract_offset_slope,
        mixing_head_matrix_slope,
        mixing_head_offset_slope,
    )


def solution(mesh):
    placed = (
        P("expert", "dp", None),
        P("expert", "dp"),
        P(("dp", "expert")),
        P("dp"),
        P(("dp", "expert"), None),
        P(),
        P(),
        P(),
        P(),
        P(),
        P(),
        P(),
        P(),
        P(),
        P(),
        P(),
        P(),
        P(),
        P(),
    )
    return jax.shard_map(
        local,
        mesh=mesh,
        in_specs=placed,
        out_specs=(
            P(("dp", "expert"), None),
            P("expert", "dp", None),
            P(),
            P("dp", None),
            P(),
            P(),
            P(),
            P(),
            P("dp", None),
            P("dp", None),
            P(),
            P("dp", None),
            P(),
            P("dp", None),
            P(),
            P("dp", None),
            P(),
        ),
        check_vma=False,
    )
```

profile of v0, /device:TPU:0, one launch (start us, length us, event | category | flops | bytes accessed | tf_op | source)
XLA Modules:
  0.0 1421.7 jit_solution(15106215308066338555)
XLA Ops:
  8.6 9.3 fusion.29
  18.0 19.2 %copy.73 = bf16[1,512,4416]{2,0,1:T(2,128)(2,1)} copy(bf16[1,512,4416]{1,2,0:T(8,128)(2,1)} %param.19) | data formatting | bytes 9043968 | tf_op args[0]
  37.6 30.7 %reduce.18 = bf16[512,4416]{1,0:T(8,128)(2,1)} reduce(bf16[512,1,4416]{2,1,0:T(2,128)(2,1)} %bitcast.133, bf16[]{:T(256)} %broadcast.246), dimensions={1}, to_apply=%bitcast.103.reduce_sub_computation | reduce | bytes 9043970
  68.3 8.0 reshape.250
  76.3 5.0 all-to-all-start
  88.4 2.7 convert_element_type.233
  91.1 2.5 reduce_sum.366
  94.3 40.2 %all-gather = bf16[4,1,128]{2,1,0:T(2,128)(2,1)S(1)} all-gather(bf16[1,1,128]{2,1,0:T(2,128)(2,1)S(1)} %convert_bitcast_fusion.1), channel_id=1, replica_groups=mesh['dp'=8,'expert'=4] {'expert'}, dimensions={0}, use_global_device_ids=true | all-gather | bytes 1280 | tf_op jit(solution)/shard_map/all_gather | solution.py:107
  144.1 9.3 all_gather.32
  160.7 9.7 all_gather.30
  170.4 2.3 copy.68
  173.5 3.1 convolution_convert_fusion.3
  178.4 3.2 convolution_add_fusion
  190.8 9.8 reshape.251
  200.5 4.2 copy.100
  206.7 5.8 copy.101
  212.5 2.9 convert.17
  215.4 11.4 fusion.3
  229.2 2.4 multiply_reduce_fusion.1
  233.4 5.6 fusion.109
  239.0 2.3 multiply_reduce_fusion.2
  245.8 3.8 convolution_convert_fusion.1
  251.9 8.7 reduce-scatter.45.cloned.1.call-start
  260.6 3.6 fusion.110
  264.2 14.4 %fusion.32 = bf16[12,64,512]{2,1,0:T(8,128)(2,1)} fusion(bf16[128,12,64]{0,2,1:T(8,128)(2,1)} %bitcast.150, f32[12,128,512]{2,1,0:T(8,128)} %fusion.110, f32[12,128,512]{2,1,0:T(8,128)} %copy-done.5, f32[12,128]{1,0:T(8,128)} %copy-done.41, pred[512]{0:T(512)(128)(4,1)} %bitcast.172), kind=kOutput, calls=%fused_computation.40 | convolution fusion | flops 109709312 | bytes 7281152 | tf_op jit(solution)/shard_map/hqk,qhd->khd/dot_general | solution.py:221
  281.0 2.9 fusion.57
  284.0 14.2 fusion.35
  299.9 6.6 reduce-scatter.45.cloned.1.call-done
  308.3 5.3 fusion.47
  314.3 6.3 fusion.43
  320.7 6.7 fusion.60
  333.6 3.9 multiply_reduce_fusion.3
  339.3 3.9 stack.45
  348.6 2.7 fusion.105
  351.4 2.5 fusion.70
  354.5 8.4 all_gather.33
  363.9 11.0 convolution_bitcast_fusion
  374.9 4.4 reduce-scatter.37.cloned.1.call-done
  386.5 2.5 concatenate.12
  389.0 4.9 all-to-all-start.1
  394.0 117.4 %reduce-scatter.35.cloned.1.call-done = f32[96,2304]{1,0:T(8,128)} async-done(((f32[768,2304]{1,0:T(8,128)}), f32[96,2304]{1,0:T(8,128)}) %reduce-scatter.35.cloned.1.call-update) | async-done | bytes 884752 | tf_op jit(solution)/shard_map/reduce_scatter | solution.py:258
  515.5 161.9 %reduce-scatter.39.cloned.1.call-done = f32[96,3072]{1,0:T(8,128)} async-done(((f32[768,3072]{1,0:T(8,128)}), f32[96,3072]{1,0:T(8,128)}) %reduce-scatter.39.cloned.1.call-update) | async-done | bytes 1179664 | tf_op jit(solution)/shard_map/reduce_scatter | solution.py:260
  679.6 164.0 %reduce-scatter.43.cloned.1.call-done = f32[384,768]{1,0:T(8,128)} async-done(((f32[3072,768]{1,0:T(8,128)}), f32[384,768]{1,0:T(8,128)}) %reduce-scatter.43.cloned.1.call-update) | async-done | bytes 1179664 | tf_op jit(solution)/shard_map/reduce_scatter | solution.py:261
  850.0 3.0 fusion.6
  854.1 120.1 %all-reduce.6.cloned.1.call-done = (f32[5]{0:T(128)}, f32[768]{0:T(1024)}, f32[8,768]{1,0:T(8,128)}, f32[3,768]{1,0:T(4,128)}, f32[3,768]{1,0:T(4,128)}, /*index...) async-done(((f32[5]{0:T(128)}, f32[768]{0:T(1024)}, f32[8,768]{1,0:T(8,128)}, f32[3,768]{1,0:T(4,128)}, f32[3,768]{1,0:T(4,128)}, /*index=5*/f32[768]{0:T(1024)}, ...) | async-done | bytes 65652 | tf_op jit(solution)/shard_map/psum | solution.py:156
  976.1 69.0 %reduce-scatter.57.cloned.1.call-done = f32[96,276]{1,0:T(8,128)} async-done(((f32[768,276]{1,0:T(8,128)}), f32[96,276]{1,0:T(8,128)}) %reduce-scatter.57.cloned.1.call-update) | async-done | bytes 106000
  1046.7 8.9 fusion
  1061.5 7.0 all-gather.2
  1070.1 199.4 %reduce-scatter.33.cloned.1.call-done = f32[552,768]{1,0:T(8,128)} async-done(((f32[4416,768]{1,0:T(8,128)}), f32[552,768]{1,0:T(8,128)}) %reduce-scatter.33.cloned.1.call-update) | async-done | bytes 1695760 | tf_op jit(solution)/shard_map/reduce_scatter | solution.py:257
  1269.4 2.4 convert_element_type.252
  1274.1 10.4 fusion.4
  1284.5 6.9 reduce-scatter.53.cloned.1.call-done
  1291.5 6.2 all_gather.36
  1299.5 16.6 %reduce-scatter.51.cloned.1.call-done = bf16[576,96]{1,0:T(8,128)(2,1)} async-done(((bf16[2304,96]{1,0:T(8,128)(2,1)}), bf16[576,96]{1,0:T(8,128)(2,1)}) %reduce-scatter.51.cloned.1.call-update) | async-done | bytes 110608
  1317.8 6.8 all-gather.1
  1325.8 2.7 reshape.223
  1328.5 12.3 reduce-scatter.41.cloned.1.call-done
  1340.9 7.3 all_gather.37
  1349.3 16.2 %reduce-scatter.55.cloned.1.call-done = bf16[192,384]{1,0:T(8,128)(2,1)} async-done(((bf16[768,384]{1,0:T(8,128)(2,1)}), bf16[192,384]{1,0:T(8,128)(2,1)}) %reduce-scatter.55.cloned.1.call-update) | async-done | bytes 147472
  1365.5 8.2 all_gather.38
  1373.7 2.3 copy.85
  1376.0 17.1 %reduce-scatter.49.cloned.1.call-done = bf16[192,552]{1,0:T(8,128)(2,1)} async-done(((bf16[768,552]{1,0:T(8,128)(2,1)}), bf16[192,552]{1,0:T(8,128)(2,1)}) %reduce-scatter.49.cloned.1.call-update) | async-done | bytes 211984
  1393.2 10.3 all_gather.34
  1403.5 2.4 copy.83
  (255 shorter events, 119.4 us)
Async XLA Ops:
  7.2 132.6 %copy-start = (bf16[768,2304]{1,0:T(8,128)(2,1)S(1)}, bf16[768,2304]{1,0:T(8,128)(2,1)}, u32[]{:S(2)}) copy-start(bf16[768,2304]{1,0:T(8,128)(2,1)} %param.29) | copy-start | bytes 10616836
  7.2 130.2 %reduce-scatter.31.cloned.1.call-start = ((), (), s32[]{:S(2)}) async-start(), calls=%async_computation.16 | async-start | bytes 1966080 | tf_op jit(solution)/shard_map/reduce_scatter | solution.py:90
  76.3 5.1 copy-start.50
  76.3 5.7 copy-start.48
  76.3 7.6 copy-start.43
  76.3 114.5 %all-to-all-start = ((bf16[4,2,282624]{2,1,0:T(2,128)(2,1)}), bf16[4,2,282624]{2,1,0:T(2,128)(2,1)}, u32[]{:S(2)}, u32[]{:S(2)}) async-start(bf16[4,2,282624]{2,1,0:T(2,128)(2,1)} %reshape.250), calls=%async_computation.1 | async-start | bytes 9043968 | tf_op jit(solution)/shard_map/all_to_all | solution.py:87
  81.3 216.9 %reduce-scatter.47.cloned.1.call-start = ((), (), s32[]{:S(2)}) async-start(), calls=%async_computation.24 | async-start | bytes 983040
  138.5 3.8 copy-start.34
  139.7 2.6 copy-start.38
  155.7 3.5 copy-start.45
  155.7 5.0 copy-start.15
  157.6 1.6 copy-start.5
  157.6 3.1 copy-start.22
  172.7 4.0 copy-start.4
  172.7 4.0 copy-start.9
  172.7 4.0 copy-start.32
  173.5 3.2 copy-start.41
  173.5 4.9 copy-start.19
  173.5 4.9 copy-start.25
  173.5 8.1 slice-start.2
  176.7 4.9 slice-start.3
  177.7 4.0 copy-start.2
  178.4 3.2 copy-start.46
  181.7 1.8 copy-start.6
  181.7 2.5 copy-start.18
  181.7 2.5 copy-start.23
  181.7 2.5 copy-start.26
  181.7 2.5 copy-start.40
  212.5 2.9 copy-start.1
  215.4 11.4 copy-start.21
  229.2 9.8 slice-start
  233.4 8.0 copy-start.11
  233.4 5.6 slice-start.1
  233.4 5.6 copy-start.3
  233.4 5.6 copy-start.29
  233.4 5.6 copy-start.36
  238.9 2.4 copy-start.12
  239.0 3.9 copy-start.10
  251.9 54.6 %reduce-scatter.45.cloned.1.call-start = ((), (), s32[]{:S(2)}) async-start(), calls=%async_computation.23 | async-start | bytes 983040
  280.9 98.4 %reduce-scatter.37.cloned.1.call-start = ((), (), s32[]{:S(2)}) async-start(), calls=%async_computation.19 | async-start | bytes 2654208 | tf_op jit(solution)/shard_map/reduce_scatter | solution.py:259
  284.0 227.4 %reduce-scatter.35.cloned.1.call-start = ((), (), s32[]{:S(2)}) async-start(), calls=%async_computation.18 | async-start | bytes 7962624 | tf_op jit(solution)/shard_map/reduce_scatter | solution.py:258
  313.6 363.7 %reduce-scatter.39.cloned.1.call-start = ((), (), s32[]{:S(2)}) async-start(), calls=%async_computation.20 | async-start | bytes 10616832 | tf_op jit(solution)/shard_map/reduce_scatter | solution.py:260
  320.7 522.9 %reduce-scatter.43.cloned.1.call-start = ((), (), s32[]{:S(2)}) async-start(), calls=%async_computation.22 | async-start | bytes 10616832 | tf_op jit(solution)/shard_map/reduce_scatter | solution.py:261
  327.4 2.1 copy-start.31
  327.4 4.0 copy-start.30
  327.4 646.8 %all-reduce.6.cloned.1.call-start = ((), (), s32[]{:S(2)}) async-start(), calls=%async_computation.30 | async-start | bytes 152576 | tf_op jit(solution)/shard_map/psum | solution.py:156
  327.7 11.0 copy-start.49
  327.7 11.0 copy-start.51
  327.7 11.0 copy-start.53
  327.7 11.0 copy-start.54
  333.6 17.8 %copy-start.24 = (f32[768]{0:T(1024)S(1)}, f32[768]{0:T(1024)}, u32[]{:S(2)}) copy-start(f32[768]{0:T(1024)} %get-tuple-element.109) | copy-start | bytes 9220
  333.6 17.8 %copy-start.27 = (f32[768]{0:T(1024)S(1)}, f32[768]{0:T(1024)}, u32[]{:S(2)}) copy-start(f32[768]{0:T(1024)} %get-tuple-element.68) | copy-start | bytes 9220
  351.3 693.8 %reduce-scatter.57.cloned.1.call-start = ((), (), s32[]{:S(2)}) async-start(), calls=%async_computation.29 | async-start | bytes 1327104
  353.9 915.6 %reduce-scatter.33.cloned.1.call-start = ((), (), s32[]{:S(2)}) async-start(), calls=%async_computation.17 | async-start | bytes 15261696 | tf_op jit(solution)/shard_map/reduce_scatter | solution.py:257
  374.9 916.6 %reduce-scatter.53.cloned.1.call-start = ((), (), s32[]{:S(2)}) async-start(), calls=%async_computation.27 | async-start | bytes 245760
  389.0 885.2 %all-to-all-start.1 = ((bf16[4,128,4416]{1,2,0:T(8,128)(2,1)}), bf16[4,128,4416]{1,2,0:T(8,128)(2,1)}, u32[]{:S(2)}, u32[]{:S(2)}) async-start(bf16[4,128,4416]{1,2,0:T(8,128)(2,1)} %concatenate.12), calls=%async_computation.2 | async-start | bytes 9043968 | tf_op jit(solution)/shard_map/all_to_all | solution.py:160
  393.9 922.2 %reduce-scatter.51.cloned.1.call-start = ((), (), s32[]{:S(2)}) async-start(), calls=%async_computation.26 | async-start | bytes 737280
  515.4 332.5 %copy-start.52 = (u32[32]{0:T(128)S(1)}, u32[32]{0:T(128)}, u32[]{:S(2)}) copy-start(u32[32]{0:T(128)} %constant.58) | copy-start | bytes 388
  515.5 825.4 %reduce-scatter.41.cloned.1.call-start = ((), (), s32[]{:S(2)}) async-start(), calls=%async_computation.21 | async-start | bytes 737280 | tf_op jit(solution)/shard_map/reduce_scatter | solution.py:274
  679.6 685.9 %reduce-scatter.55.cloned.1.call-start = ((), (), s32[]{:S(2)}) async-start(), calls=%async_computation.28 | async-start | bytes 737280
  847.9 545.3 %reduce-scatter.49.cloned.1.call-start = ((), (), s32[]{:S(2)}) async-start(), calls=%async_computation.25 | async-start | bytes 1228800
  1056.3 2.5 collective-permute-start
  1365.5 46.9 %copy-start.37 = (f32[3072]{0:T(1024)S(1)}, f32[3072]{0:T(1024)}, u32[]{:S(2)}) copy-start(f32[3072]{0:T(1024)} %get-tuple-element.126) | copy-start | bytes 36868
  1365.5 47.5 %copy-start.47 = (f32[768]{0:T(1024)S(1)}, f32[768]{0:T(1024)}, u32[]{:S(2)}) copy-start(f32[768]{0:T(1024)} %get-tuple-element.128) | copy-start | bytes 9220
  (13 other events, 9.9 us)
Sparse Core Ops, SparseCore 0:
  18.1 30.8 reduce-scatter.30
  252.0 25.4 reduce-scatter.46
  281.1 25.4 reduce-scatter.44
  310.3 68.9 reduce-scatter.36
  383.3 128.0 reduce-scatter.34
  514.8 162.5 reduce-scatter.38
  681.0 162.5 reduce-scatter.42
  851.7 122.4 all-reduce.5
  978.6 66.4 reduce-scatter.56
  1048.9 220.4 reduce-scatter.32
  1272.6 18.8 reduce-scatter.52
  1294.0 22.0 reduce-scatter.50
  1318.7 22.0 reduce-scatter.40
  1343.4 22.0 reduce-scatter.54
  1368.7 24.4 reduce-scatter.48
where the time goes:
time: 1430 us; the launch traced here: 1420 us
  waiting for transfers between devices  912 us (64%)
  local copies, waits for them, and re-layouts  130 us (9%)
  blocking collectives  122 us (9%)
  matrix products  120 us (8%)
  other arithmetic  100 us (7%)
  starting transfers between devices  20.8 us (1%)
  between operations  17 us (1%)
    reduce_scatter x1, waiting for transfers between devices, local(): lax.psum_scatter(lift_matrix_derivative, 'dp', scatter_dimension=0, tiled...  199 us
    reduce_scatter x1, waiting for transfers between devices, local(): lax.psum_scatter(weight_reduce_grad, 'dp', scatter_dimension=0, tiled=True)  164 us
    reduce_scatter x1, waiting for transfers between devices, local(): lax.psum_scatter(weight_expand_grad, 'dp', scatter_dimension=0, tiled=True)  162 us
    unnamed x23, waiting for transfers between devices  133 us
    psum x1, waiting for transfers between devices, local(): stat_total = lax.psum(stat_local, ('dp', 'expert'))  120 us
    reduce_scatter x1, waiting for transfers between devices, local(): lax.psum_scatter(weight_in_grad, 'dp', scatter_dimension=0, tiled=True)  117 us
    unnamed x149, local copies, waits for them, and re-layouts  93.3 us
    all_gather x1, blocking collectives, local(): lax.all_gather(piece_usable_flags.astype(jnp.bfloat16), 'expert', axis=0,...  40.2 us
  transfers between devices with their start and end apart: 18, of which 13 were waited for; matrix products, arithmetic and copies ran while one was open for 19% of the time, Pallas kernels for 0%

commit v1 on v0

v1 whole, which is shorter than its diff:
```python
import jax
import jax.numpy as jnp
from jax import lax
from jax.sharding import PartitionSpec as P

D = 768
HEADS = 12
HEAD_DIM = 64
MODEL_TALLY = 3
CHANNELS = 69
PIXELS = 64
TILE_ENTRIES = 4416

NORM_EPSILON = 1e-05
SQUARE_EPSILON = 1e-06
MASKED_SCORE = -1e30
F32 = jnp.float32
BF16 = jnp.bfloat16


def normalize(values, gain_row, offset_row):
    center = values - jnp.mean(values, axis=-1, keepdims=True)
    inverse = lax.rsqrt(jnp.mean(center * center, axis=-1, keepdims=True) + NORM_EPSILON)
    unit_rows = center * inverse
    return (unit_rows * gain_row + offset_row, unit_rows, inverse)


def normalize_back(grad_out, unit_rows, inverse, gain_row):
    scaled = grad_out * gain_row
    grad_in = inverse * (
        scaled
        - jnp.mean(scaled, axis=-1, keepdims=True)
        - unit_rows * jnp.mean(scaled * unit_rows, axis=-1, keepdims=True)
    )
    return (grad_in, jnp.sum(grad_out * unit_rows, axis=0), jnp.sum(grad_out, axis=0))


def dot_nn(a, b):
    return jnp.dot(a, b, preferred_element_type=F32)


def dot_tn(a, b):
    return lax.dot_general(a, b, (((0,), (0,)), ((), ())), preferred_element_type=F32)


def dot_nt(a, b):
    return lax.dot_general(a, b, (((1,), (1,)), ((), ())), preferred_element_type=F32)


def expert_swap(v, k):
    size = lax.axis_size("expert")
    return lax.ppermute(v, "expert", [(i, i ^ k) for i in range(size)])


def frame_swap(v, k):
    size = lax.axis_size("dp")
    return lax.ppermute(v, "dp", [(i, i ^ k) for i in range(size)])


def gather_four(v):
    across = expert_swap(v, 2)
    pair = jnp.stack([v, across])
    other = expert_swap(pair, 1)
    return [v, other[0], across, other[1]]


def in_order(parts, e):
    odd = (e & 1) == 1
    high = (e & 2) == 2
    a, b, c, d = parts
    a, b, c, d = (
        jnp.where(odd, b, a),
        jnp.where(odd, a, b),
        jnp.where(odd, d, c),
        jnp.where(odd, c, d),
    )
    return [jnp.where(high, c, a), jnp.where(high, d, b), jnp.where(high, a, c), jnp.where(high, b, d)]


def frame_scatter(blocks):
    n, rows, cols = blocks.shape
    steps = n.bit_length() - 1
    me = lax.axis_index("dp")
    now = blocks.reshape((2,) * steps + (rows, cols))
    for i in range(steps):
        bit = (me >> i) & 1
        axis = steps - 1 - i
        send = lax.dynamic_index_in_dim(now, 1 - bit, axis, keepdims=False)
        keep = lax.dynamic_index_in_dim(now, bit, axis, keepdims=False)
        got = frame_swap(send, 1 << i)
        now = (keep.astype(F32) + got.astype(F32)).astype(BF16)
    return now


def frame_sum(v):
    steps = lax.axis_size("dp").bit_length() - 1
    for i in range(steps):
        v = v + frame_swap(v, 1 << i)
    return v


def square_sum(values, valid_rows):
    return jnp.sum(jnp.sum(values * values, axis=-1) * valid_rows)


def local(
    model_predictions,
    member_tile_presence,
    piece_usable_flags,
    horizon_positions,
    result_adjoint,
    tile_lift_matrix,
    tile_lift_offset,
    horizon_lookup,
    normalizer_scales,
    normalizer_offsets,
    query_key_value_matrix,
    attend_result_matrix,
    attend_offset_vector,
    expand_matrix,
    expand_offset,
    contract_matrix,
    contract_offset,
    mixing_head_matrix,
    mixing_head_offset,
):
    n = lax.axis_size("dp")
    e = lax.axis_index("expert")
    core = e & 1
    active = (e < MODEL_TALLY).astype(F32)
    pred = model_predictions[0]
    tokens = pred.shape[0]
    own = result_adjoint.shape[0]
    half = tokens // 2
    block_rows = TILE_ENTRIES // n
    step = block_rows // 4 // 8 * 8 if block_rows % 8 == 0 else block_rows // 4
    width = block_rows - 3 * step

    mask = member_tile_presence[0].astype(F32) * active
    info = jnp.concatenate([mask, piece_usable_flags.astype(F32)])[None]
    infos = in_order(gather_four(info), e)
    masks = [v[0, :tokens] for v in infos]
    valid = jnp.concatenate([v[0, tokens:] for v in infos])

    adjoints = in_order(gather_four(result_adjoint), e)
    adjoint = jnp.concatenate(adjoints, axis=0)

    part = (dot_nn(pred, tile_lift_matrix) * mask[:, None]).astype(BF16)
    other = expert_swap(part, 1)
    pair_sum = (part.astype(F32) + other.astype(F32)).astype(BF16)
    across = expert_swap(lax.dynamic_slice_in_dim(pair_sum, core * half, half, 0), 2)
    across_other = expert_swap(across, 1)
    far = jnp.where(
        core == 0,
        jnp.concatenate([across, across_other], axis=0),
        jnp.concatenate([across_other, across], axis=0),
    )
    stream_in = pair_sum.astype(F32) + far.astype(F32) + tile_lift_offset.astype(F32)

    blocked = pred.reshape(tokens, n, block_rows)
    pieces = [
        blocked[:, :, q * step : q * step + width].reshape(tokens, n * width) for q in range(4)
    ]
    pieces = in_order(pieces, e)
    columns = [pieces[0]] + [expert_swap(pieces[k], k) for k in (1, 2, 3)]
    columns = in_order(columns, e)[:MODEL_TALLY]

    gain_rows = normalizer_scales.astype(F32)
    shift_rows = normalizer_offsets.astype(F32)
    lead_hot = (jnp.arange(horizon_lookup.shape[0]) == horizon_positions[0]).astype(BF16)
    lead_vector = dot_nn(lead_hot, horizon_lookup)
    normed, unit_one, inverse_one = normalize(stream_in, gain_rows[0], shift_rows[0])
    normed_one = (normed + lead_vector).astype(BF16)
    triple = dot_nn(normed_one, query_key_value_matrix).astype(BF16)
    queries = triple[:, :D].reshape(tokens, HEADS, HEAD_DIM)
    keys_all = triple[:, D : 2 * D].reshape(tokens, HEADS, HEAD_DIM)
    values_all = triple[:, 2 * D :].reshape(tokens, HEADS, HEAD_DIM)

    def masked_scores():
        raw = jnp.einsum("qhd,khd->hqk", queries, keys_all, preferred_element_type=F32)
        return jnp.where(valid[None, None, :] > 0, raw * HEAD_DIM ** (-0.5), MASKED_SCORE)

    scores = masked_scores()
    maxima = jnp.max(scores, axis=-1, keepdims=True)
    log_norm = maxima + jnp.log(jnp.sum(jnp.exp(scores - maxima), axis=-1, keepdims=True))
    chance = jnp.exp(scores - log_norm)
    mixed = jnp.einsum("hqk,khd->qhd", chance.astype(BF16), values_all, preferred_element_type=F32)
    mixed = mixed.astype(BF16).reshape(tokens, D)
    attend_out = dot_nn(mixed, attend_result_matrix) + attend_offset_vector.astype(F32)
    stream_mid = stream_in + attend_out
    normed, unit_two, inverse_two = normalize(stream_mid, gain_rows[1], shift_rows[1])
    normed_two = normed.astype(BF16)
    hidden = dot_nn(normed_two, expand_matrix) + expand_offset.astype(F32)
    activated = jax.nn.gelu(hidden).astype(BF16)
    feed_out = dot_nn(activated, contract_matrix) + contract_offset.astype(F32)
    stream_out = stream_mid + feed_out
    normed, unit_three, inverse_three = normalize(stream_out, gain_rows[2], shift_rows[2])
    normed_three = normed.astype(BF16)
    head_vals = dot_nn(normed_three, mixing_head_matrix) + mixing_head_offset.astype(F32)
    logits = head_vals[:, : MODEL_TALLY * CHANNELS].reshape(tokens, MODEL_TALLY, CHANNELS)
    shift_out = head_vals[:, MODEL_TALLY * CHANNELS :]
    powers = jnp.exp(logits - jnp.max(logits, axis=1, keepdims=True))
    blend = powers / jnp.sum(powers, axis=1, keepdims=True)

    place = jnp.arange(n * width)
    channel = ((place // width) * block_rows + e * step + place % width) // PIXELS
    spread = (jnp.arange(CHANNELS)[:, None] == channel[None, :]).astype(F32)

    def wide(v, spread):
        return jnp.dot(v, spread, precision=lax.Precision.HIGHEST)

    combined = wide(shift_out, spread)
    for q in range(MODEL_TALLY):
        combined = combined + wide(blend[:, q], spread) * columns[q].astype(F32)
    combined = combined.astype(BF16).reshape(4, own, n * width)
    outgoing = in_order([combined[k] for k in range(4)], e)
    arrived = [outgoing[0]] + [expert_swap(outgoing[k], k) for k in (1, 2, 3)]
    arrived = [v.reshape(own, n, width) for v in in_order(arrived, e)]
    combined_prediction = jnp.concatenate(
        [v[:, :, :step] for v in arrived[:3]] + [arrived[3]], axis=2
    ).reshape(own, TILE_ENTRIES)

    adjoint_wide = adjoint.astype(F32)
    mine = jnp.sum(
        (adjoint_wide * pred.astype(F32)).reshape(tokens, CHANNELS, PIXELS), axis=-1
    )
    grad_weights = jnp.stack(in_order(gather_four(mine), e)[:MODEL_TALLY], axis=1)
    grad_shift = jnp.sum(adjoint_wide.reshape(tokens, CHANNELS, PIXELS), axis=-1)
    grad_logits = blend * (grad_weights - jnp.sum(blend * grad_weights, axis=1, keepdims=True))
    grad_head = jnp.concatenate([grad_logits.reshape(tokens, MODEL_TALLY * CHANNELS), grad_shift], axis=1)
    head_bias_grad = jnp.sum(grad_head, axis=0)
    head_low = grad_head.astype(BF16)

    def quarter(v):
        cols = v.shape[1] // 4
        return lax.dynamic_slice_in_dim(v, e * cols, cols, 1)

    def by_frame(g):
        return g.astype(BF16).reshape(n, g.shape[0] // n, g.shape[1])

    head_share = by_frame(dot_tn(normed_three, quarter(head_low)))
    grad_normed_three = dot_nt(head_low, mixing_head_matrix)
    grad_stream_out, gain_three, shift_three = normalize_back(
        grad_normed_three, unit_three, inverse_three, gain_rows[2]
    )
    contract_bias_grad = jnp.sum(grad_stream_out, axis=0)
    feed_low = grad_stream_out.astype(BF16)
    contract_share = by_frame(dot_tn(activated, quarter(feed_low)))
    grad_activated = dot_nt(feed_low, contract_matrix)
    _, gelu_back = jax.vjp(jax.nn.gelu, hidden)
    grad_hidden = gelu_back(grad_activated)[0]
    expand_bias_grad = jnp.sum(grad_hidden, axis=0)
    hidden_low = grad_hidden.astype(BF16)
    expand_share = by_frame(dot_tn(normed_two, quarter(hidden_low)))
    grad_normed_two = dot_nt(hidden_low, expand_matrix)
    grad_mid_norm, gain_two, shift_two = normalize_back(
        grad_normed_two, unit_two, inverse_two, gain_rows[1]
    )
    grad_stream_mid = grad_stream_out + grad_mid_norm
    attend_bias_grad = jnp.sum(grad_stream_mid, axis=0)
    attend_low = grad_stream_mid.astype(BF16)
    result_share = by_frame(dot_tn(mixed, quarter(attend_low)))
    grad_mixed = dot_nt(attend_low, attend_result_matrix).astype(BF16).reshape(tokens, HEADS, HEAD_DIM)
    grad_values = jnp.einsum("hqk,qhd->khd", chance.astype(BF16), grad_mixed, preferred_element_type=F32)
    grad_chance = jnp.einsum("qhd,khd->hqk", grad_mixed, values_all, preferred_element_type=F32)
    delta_rows = jnp.sum(chance * grad_chance, axis=-1, keepdims=True)
    grad_scores = (chance * (grad_chance - delta_rows) * HEAD_DIM ** (-0.5)).astype(BF16)
    grad_queries = jnp.einsum("hqk,khd->qhd", grad_scores, keys_all, preferred_element_type=F32)
    grad_keys = jnp.einsum("hqk,qhd->khd", grad_scores, queries, preferred_element_type=F32)
    grad_triple = jnp.concatenate(
        [v.reshape(tokens, D) for v in (grad_queries, grad_keys, grad_values)], axis=1
    ).astype(BF16)
    triple_share = by_frame(dot_tn(normed_one, quarter(grad_triple)))
    grad_normed_one = dot_nt(grad_triple, query_key_value_matrix)
    lead_grad = lead_hot.astype(F32)[:, None] * jnp.sum(grad_normed_one, axis=0)[None, :]
    grad_in_norm, gain_one, shift_one = normalize_back(
        grad_normed_one, unit_one, inverse_one, gain_rows[0]
    )
    grad_stream_in = grad_stream_mid + grad_in_norm
    lift_bias_grad = jnp.sum(grad_stream_in, axis=0)
    embed_low = grad_stream_in.astype(BF16)

    lift_part = 0.0
    for q in range(MODEL_TALLY):
        lift_part = lift_part + dot_tn(columns[q], embed_low * masks[q].astype(BF16)[:, None])
    lift_share = lift_part.astype(BF16).reshape(n, width, D)

    own_blend = jnp.where(e == 0, blend[:, 0], jnp.where(e == 1, blend[:, 1], blend[:, 2])) * active
    natural = (
        jnp.arange(CHANNELS)[:, None] == (jnp.arange(TILE_ENTRIES) // PIXELS)[None, :]
    ).astype(F32)
    predictions_slope = (
        dot_nt(embed_low * mask.astype(BF16)[:, None], tile_lift_matrix)
        + wide(own_blend, natural) * adjoint_wide
    ).astype(BF16)[None]

    def finish(share):
        return in_order(gather_four(frame_scatter(share)), e)

    def columns_of(share):
        return jnp.concatenate(finish(share), axis=1).astype(F32)

    head_slope = columns_of(head_share)
    contract_slope = columns_of(contract_share)
    expand_slope = columns_of(expand_share)
    result_slope = columns_of(result_share)
    triple_slope = columns_of(triple_share)
    lift_rows = finish(lift_share)
    lift_slope = jnp.concatenate([v[:step] for v in lift_rows[:3]] + [lift_rows[3]], axis=0).astype(F32)

    stats = jnp.stack(
        [square_sum(v, valid) for v in (stream_in, attend_out, feed_out, stream_out)] + [jnp.sum(valid)]
    )
    flat = [
        lift_bias_grad,
        lead_grad,
        jnp.stack([gain_one, gain_two, gain_three]),
        jnp.stack([shift_one, shift_two, shift_three]),
        attend_bias_grad,
        expand_bias_grad,
        contract_bias_grad,
        head_bias_grad,
        stats,
    ]
    sizes = [v.size for v in flat]
    packed = jnp.concatenate([v.reshape(-1) for v in flat])
    packed = jnp.pad(packed, (0, -packed.size % 1024)).reshape(-1, 128)
    packed = frame_sum(packed).reshape(-1)
    back, at = [], 0
    for v, size in zip(flat, sizes):
        back.append(packed[at : at + size].reshape(v.shape))
        at += size
    total = back[8]
    magnitudes = jnp.sqrt(total[:4] / (total[4] * D) + SQUARE_EPSILON)
    return (
        combined_prediction,
        predictions_slope,
        magnitudes,
        lift_slope,
        back[0],
        back[1],
        back[2],
        back[3],
        triple_slope,
        result_slope,
        back[4],
        expand_slope,
        back[5],
        contract_slope,
        back[6],
        head_slope,
        back[7],
    )


def solution(mesh):
    rows = P(("dp", "expert"), None)
    placed = (
        P("expert", "dp", None),
        P("expert", "dp"),
        P(("dp", "expert")),
        P("dp"),
        rows,
    ) + (P(),) * 14
    given = (
        rows,
        P("expert", "dp", None),
        P(),
        P("dp", None),
        P(),
        P(),
        P(),
        P(),
        P("dp", None),
        P("dp", None),
        P(),
        P("dp", None),
        P(),
        P("dp", None),
        P(),
        P("dp", None),
        P(),
    )
    return jax.shard_map(local, mesh=mesh, in_specs=placed, out_specs=given, check_vma=False)
```

time: 1430 us -> 535 us (0.37)
  waiting for transfers between devices: 912 us -> 81.7 us
  blocking collectives: 122 us -> 0 us
  matrix products: 120 us -> 158 us
  starting transfers between devices: 20.8 us -> 46.7 us
  other arithmetic: 100 us -> 116 us
    reduce_scatter x7 -> x0, waiting for transfers between devices: 659 us -> none  [the longest x1 199 us: local(): lax.psum_scatter(lift_matrix_derivative, 'dp', scatter_dimension=0, tiled...]
    unnamed x23 -> x0, waiting for transfers between devices: 133 us -> none
    psum x1 -> x0, waiting for transfers between devices: 120 us -> none  [local(): stat_total = lax.psum(stat_local, ('dp', 'expert'))]
    all_gather x10 -> x0, blocking collectives: 114 us -> none  [the longest x1 40.2 us: local(): lax.all_gather(piece_usable_flags.astype(jnp.bfloat16), 'expert', axis=0,...]
    ppermute x0 -> x48, waiting for transfers between devices: none -> 81.7 us  [the longest x27 47.8 us: expert_swap(): return lax.ppermute(v, 'expert', [(i, i ^ k) for i in range(size)])]
    unnamed x149 -> x256, local copies, waits for them, and re-layouts: 93.3 us -> 18.8 us
    ppermute x0 -> x48, starting transfers between devices: none -> 46.7 us  [the longest x21 31 us: frame_swap(): return lax.ppermute(v, 'dp', [(i, i ^ k) for i in range(size)])]
    unnamed x4, other arithmetic: 31.3 us -> 0.01 us
  transfers between devices with their start and end apart: 18 -> 48, of which waited for: 13 -> 18; matrix products, arithmetic and copies ran while one was open for 19% -> 47% of each run, Pallas kernels for 0% -> 0%
where the time goes in v1:
time: 535 us; the launch traced here: 528 us
  matrix products  158 us (30%)
  local copies, waits for them, and re-layouts  119 us (22%)
  other arithmetic  116 us (22%)
  waiting for transfers between devices  81.7 us (15%)
  starting transfers between devices  46.7 us (9%)
  between operations  6.33 us (1%)
    ppermute x27, waiting for transfers between devices, expert_swap(): return lax.ppermute(v, 'expert', [(i, i ^ k) for i in range(size)])  47.8 us
    ppermute x21, waiting for transfers between devices, frame_swap(): return lax.ppermute(v, 'dp', [(i, i ^ k) for i in range(size)])  33.9 us
    ppermute x21, starting transfers between devices, frame_swap(): return lax.ppermute(v, 'dp', [(i, i ^ k) for i in range(size)])  31 us
    dot_general x6, matrix products, dot_nt(): lax.dot_general(a, b, (((1,), (1,)), ((), ())), preferred_element_type=F32)  29.2 us
    dot_general x7, matrix products, dot_nn(): return jnp.dot(a, b, preferred_element_type=F32)  27.6 us
    dot_general x1, matrix products, local(): jnp.einsum('hqk,qhd->khd', grad_scores, queries, preferred_element_type=F32)  24.3 us
    dot_general x1, matrix products, local(): jnp.einsum('hqk,khd->qhd', grad_scores, keys_all, preferred_element_type=...  23.5 us
    unnamed x256, local copies, waits for them, and re-layouts  18.8 us
  transfers between devices with their start and end apart: 48, of which 18 were waited for; matrix products, arithmetic and copies ran while one was open for 47% of the time, Pallas kernels for 0%

profile of v1, /device:TPU:0, one launch (start us, length us, event | category | flops | bytes accessed | tf_op | source)
XLA Modules:
  0.0 527.8 jit_solution(9350454998747677923)
XLA Ops:
  1.5 9.2 %multiply_convert_fusion.2 = bf16[512,768]{1,0:T(8,128)(2,1)} fusion(bf16[4416,768]{1,0:T(8,128)(2,1)} %param.24, bf16[1,512,4416]{1,2,0:T(8,128)(2,1)} %param.19, f32[512]{0:T(512)S(1)} %bitcast.541), kind=kOutput, calls=%fused_computation.67 | convolution fusion | flops 3473670144 | bytes 12093440 | tf_op jit(solution)/shard_map/dot_general | solution.py:39
  12.9 2.5 collective-permute-start.3
  15.4 5.1 broadcast_select_fusion.7
  20.6 2.5 copy.97
  24.7 2.4 copy.98
  43.4 2.4 copy.99
  45.7 2.4 copy.100
  61.1 3.3 pad_maximum_fusion.2
  64.4 37.2 %collective-permute-done.1 = bf16[256,768]{1,0:T(8,128)(2,1)S(1)} collective-permute-done((bf16[256,768]{1,0:T(8,128)(2,1)S(1)}, bf16[256,768]{1,0:T(8,128)(2,1)S(1)}, u32[]{:S(2)}, u32[]{:S(2)}) %collective-permute-start.1) | collective-permute-done | bytes 393248 | tf_op jit(solution)/shard_map/ppermute | solution.py:52
  101.7 4.2 broadcast_select_fusion.8
  107.6 2.4 convolution_convert_fusion
  111.5 2.4 copy.94
  113.9 2.3 copy.95
  116.2 4.5 fusion.2
  120.7 2.6 exponential_reduce_fusion
  125.3 9.9 %fusion.6 = bf16[12,512,512]{1,2,0:T(8,128)(2,1)} fusion(f32[12,512,512]{1,2,0:T(8,128)} %copy-done.1, f32[12,512]{1,0:T(8,128)S(1)} %log_add_fusion, pred[512]{0:T(512)(128)(4,1)S(1)} %copy-done.93), kind=kLoop, calls=%fused_computation.14 | loop fusion | flops 12582912 | bytes 18899456 | tf_op jit(solution)/shard_map/convert_element_type | solution.py:187
  135.2 2.3 copy.93
  137.6 4.3 convolution_convert_fusion.6
  144.6 8.8 %multiply_convert_fusion.1 = (bf16[512,3072]{1,0:T(8,128)(2,1)S(1)}, f32[512,3072]{1,0:T(8,128)}) fusion(f32[3072]{0:T(1024)S(1)} %copy-done.88, bf16[768,3072]{1,0:T(8,128)(2,1)} %param.32, f32[512,768]{1,0:T(8,128)S(1)} %get-tuple-element.81, f32[768]{0:T(1024)S(1)} %copy-done.112, f32[768]{0:T(1024)S(1)} %copy-done.83, f32[512]{0:T(512)S(1)} %add_rsqrt_fusion.1, ...), kind=kOutput, calls=%fused_computation.23 | convolution fusion | flops 2433613824 | bytes 15751168 | tf_op jit(solution)/shard_map/dot_general | solution.py:39
  153.5 3.4 fusion.158
  157.3 2.9 broadcast_select_fusion.19
  161.1 6.4 %fusion.3 = (f32[512,69]{0,1:T(8,128)S(1)}, f32[512,69]{0,1:T(8,128)}) fusion(bf16[512,69,64]{0,2,1:T(8,128)(2,1)S(1)} %bitcast.493, bf16[128,69,64]{0,2,1:T(8,128)(2,1)S(1)} %bitcast.508, bf16[128,69,64]{0,2,1:T(8,128)(2,1)S(1)} %bitcast.507, bf16[128,69,64]{0,2,1:T(8,128)(2,1)S(1)} %bitcast.506, bf16[128,69,64]{0,2,1:T(8,128)(2,1)S(1)} %bitcast.505), kind=kLoop, calls=%fused_computation.12 | loop fusion | flops 27061248 | bytes 9326592 | tf_op jit(solution)/shard_map/reduce_sum | solution.py:224
  168.3 5.4 %collective-permute-done.13 = f32[512,69]{0,1:T(8,128)S(1)} collective-permute-done((f32[512,69]{0,1:T(8,128)S(1)}, f32[512,69]{0,1:T(8,128)S(1)}, u32[]{:S(2)}, u32[]{:S(2)}) %collective-permute-start.13) | collective-permute-done | bytes 141344 | tf_op jit(solution)/shard_map/ppermute | solution.py:52
  189.4 2.0 multiply_reduce_fusion.17
  202.3 9.2 %fusion.153 = (f32[3072]{0:T(1024)}, bf16[512,3072]{1,0:T(8,128)(2,1)S(1)}) fusion(f32[512,3072]{1,0:T(8,128)} %get-tuple-element.166, f32[3072]{0:T(1024)S(1)} %copy-done.89, bf16[512,768]{1,0:T(8,128)(2,1)S(1)} %convert_element_type.474, bf16[3072,768]{1,0:T(8,128)(2,1)S(1)} %bitcast.549), kind=kOutput, calls=%fused_computation.436 | convolution fusion | flops 2450519040 | bytes 14966784 | tf_op jit(solution)/shard_map/dot_general | solution.py:47
  211.6 3.5 multiply_reduce_fusion.6
  221.0 2.3 copy.106
  223.3 7.8 %fusion.163 = f32[12,512,512]{1,2,0:T(8,128)} fusion(bf16[512,12,64]{0,2,1:T(8,128)(2,1)} %bitcast.497, bf16[512,12,64]{0,2,1:T(8,128)(2,1)} %bitcast.495), kind=kOutput, calls=%fused_computation.443 | convolution fusion | flops 402653184 | bytes 14155776 | tf_op jit(solution)/shard_map/qhd,khd->hqk/dot_general | solution.py:265
  231.1 23.5 %fusion.43 = bf16[12,64,512]{2,1,0:T(8,128)(2,1)} fusion(bf16[512,12,64]{0,2,1:T(8,128)(2,1)} %bitcast.514, f32[12,512,512]{1,2,0:T(8,128)} %fusion.163, f32[12,512,512]{1,2,0:T(8,128)} %copy-done.1, f32[12,512]{1,0:T(8,128)} %copy-done.69, pred[512]{0:T(512)(128)(4,1)} %broadcast_compare_fusion), kind=kOutput, calls=%fused_computation.76 | convolution fusion | flops 437656064 | bytes 26763776 | tf_op jit(solution)/shard_map/hqk,khd->qhd/dot_general | solution.py:268
  254.6 24.3 %fusion.46 = bf16[12,64,512]{2,1,0:T(8,128)(2,1)} fusion(bf16[512,12,64]{0,2,1:T(8,128)(2,1)} %bitcast.512, f32[12,512,512]{1,2,0:T(8,128)} %fusion.163, f32[12,512,512]{1,2,0:T(8,128)} %copy-done.1, f32[12,512]{1,0:T(8,128)} %copy-done.69, pred[512]{0:T(512)(128)(4,1)} %broadcast_compare_fusion), kind=kOutput, calls=%fused_computation.77 | convolution fusion | flops 437656064 | bytes 26763776 | tf_op jit(solution)/shard_map/hqk,qhd->khd/dot_general | solution.py:269
  278.8 6.0 %convolution_convert_fusion.5 = bf16[12,64,512]{2,1,0:T(8,128)(2,1)} fusion(bf16[512,12,64]{0,2,1:T(8,128)(2,1)} %bitcast.498, bf16[12,512,512]{1,2,0:T(8,128)(2,1)} %fusion.6), kind=kOutput, calls=%fused_computation.78 | convolution fusion | flops 403046400 | bytes 7864320 | tf_op jit(solution)/shard_map/hqk,qhd->khd/dot_general | solution.py:264
  285.6 2.6 fusion.78
  288.2 2.5 fusion.79
  290.7 2.5 fusion.77
  300.8 4.0 reshape_reshape.22
  304.8 5.1 constant_dynamic-slice_fusion.3
  311.6 2.2 convolution_convert_fusion.2
  315.5 2.2 reshape_reshape.20
  317.7 2.8 constant_dynamic-slice_fusion.7
  323.6 2.0 copy.127
  325.6 6.6 %multiply_reduce_fusion.7 = (f32[768]{0:T(1024)}, f32[512]{0:T(512)S(1)}, f32[512]{0:T(512)S(1)}, f32[768]{0:T(1024)S(1)}, f32[512,768]{1,0:T(8,128)}) fusion(f32[512]{0:T(512)} %copy-done.91, f32[512]{0:T(512)S(1)} %copy-done.76, f32[768]{0:T(1024)S(1)} %convert_element_type.450, bf16[256,768]{1,0:T(8,128)(2,1)} %copy-done.38, ...), kind=kOutput, calls=%fused_computation.52 | convolution fusion | flops 1827665408 | bytes 9064449 | tf_op jit(solution)/shard_map/dot_general | solution.py:47
  343.5 4.9 fusion.156
  348.3 4.1 concatenate.111
  354.6 6.4 %fusion.60 = f32[512,4416]{0,1:T(8,128)S(1)} fusion(bf16[4416,768]{1,0:T(8,128)(2,1)} %param.24, bf16[512,768]{1,0:T(8,128)(2,1)} %get-tuple-element.72, bf16[512]{0:T(512)(128)(2,1)} %convert_element_type.480), kind=kOutput, calls=%fused_computation.131 | convolution fusion | flops 3473276928 | bytes 16614400 | tf_op jit(solution)/shard_map/dot_general | solution.py:47
  365.8 2.9 add_convert_fusion.1
  372.2 7.6 %fusion.35 = bf16[1,512,4416]{1,2,0:T(8,128)(2,1)} fusion(f32[512,4416]{0,1:T(8,128)S(1)} %fusion.60, bf16[128,4416]{0,1:T(8,128)(2,1)S(1)} %copy-done.33, bf16[128,4416]{0,1:T(8,128)(2,1)S(1)} %copy-done.31, bf16[128,4416]{0,1:T(8,128)(2,1)S(1)} %copy-done.29, bf16[128,4416]{0,1:T(8,128)(2,1)S(1)} %copy-done.27, s32[4416]{0:T(1024)S(1)} %copy-done.74, ...), kind=kOutput, calls=%fused_computation.32 | convolution fusion | flops 1897382912 | bytes 18529542 | tf_op jit(solution)/shard_map/dot_general | solution.py:210
  386.9 2.6 collective-permute-start.45
  390.8 2.2 copy.112
  402.5 2.1 collective-permute-done.16
  408.6 2.9 collective-permute-done.17
  433.1 2.4 broadcast_select_fusion.33
  448.1 2.4 pad_maximum_fusion.3
  452.2 3.2 collective-permute-done.23
  461.2 5.7 %collective-permute-done.24 = bf16[2,96,576]{2,1,0:T(8,128)(2,1)S(1)} collective-permute-done((bf16[2,96,576]{2,1,0:T(8,128)(2,1)S(1)}, bf16[2,96,576]{2,1,0:T(8,128)(2,1)S(1)}, u32[]{:S(2)}, u32[]{:S(2)}) %collective-permute-start.24) | collective-permute-done | bytes 221216 | tf_op jit(solution)/shard_map/ppermute | solution.py:57
  468.1 2.6 collective-permute-start.34
  470.6 4.4 collective-permute-done.25
  479.5 2.4 collective-permute-start.35
  489.3 2.0 concatenate.113
  491.4 2.1 convert_element_type.515
  497.5 2.8 collective-permute-start.20
  501.3 9.7 %collective-permute-done.20 = bf16[144,768]{1,0:T(8,128)(2,1)S(1)} collective-permute-done((bf16[144,768]{1,0:T(8,128)(2,1)S(1)}, bf16[144,768]{1,0:T(8,128)(2,1)S(1)}, u32[]{:S(2)}, u32[]{:S(2)}) %collective-permute-start.20) | collective-permute-done | bytes 221216 | tf_op jit(solution)/shard_map/ppermute | solution.py:57
  514.4 3.7 collective-permute-done.21
  520.1 2.7 copy.121
  522.8 2.3 maximum_convert_fusion.1
  (513 shorter events, 197.6 us)
Async XLA Ops:
  0.7 106.9 %copy-start = (bf16[768,2304]{1,0:T(8,128)(2,1)S(1)}, bf16[768,2304]{1,0:T(8,128)(2,1)}, u32[]{:S(2)}) copy-start(bf16[768,2304]{1,0:T(8,128)(2,1)} %param.29) | copy-start | bytes 10616836
  1.5 10.2 %copy-start.73 = (f32[1,512]{1,0:T(1,128)}, f32[1,512]{1,0:T(1,128)S(1)}, u32[]{:S(2)}) copy-start(f32[1,512]{1,0:T(1,128)S(1)} %convert_multiply_fusion.1) | copy-start | bytes 6148
  1.5 9.7 %copy-start.117 = (s32[128]{0:T(128)S(1)}, s32[128]{0:T(128)}, u32[]{:S(2)}) copy-start(s32[128]{0:T(128)} %param.21) | copy-start | bytes 1540
  10.8 47.1 %collective-permute-start = (bf16[512,768]{1,0:T(8,128)(2,1)}, bf16[512,768]{1,0:T(8,128)(2,1)}, u32[]{:S(2)}, u32[]{:S(2)}) collective-permute-start(bf16[512,768]{1,0:T(8,128)(2,1)} %multiply_convert_fusion.2), channel_id=1, source_target_pairs={{0,1},{1,0},{2,3},{3,2},{4,5},{5,4},{6,7},{7,6},{8,9},{9,8},{10,11... | collective-permute-start | bytes 2359304 | tf_op jit(solution)/shard_map/ppermute | solution.py:52
  12.9 21.5 %collective-permute-start.3 = (f32[1,640]{1,0:T(1,128)}, f32[1,640]{1,0:T(1,128)}, u32[]{:S(2)}, u32[]{:S(2)}) collective-permute-start(f32[1,640]{1,0:T(1,128)} %broadcast_in_dim.18), channel_id=1, source_target_pairs={{0,2},{1,3},{2,0},{3,1},{4,6},{5,7},{6,4},{7,5},{8,10},{9,11},{10,... | collective-permute-start | bytes 7688 | tf_op jit(solution)/shard_map/ppermute | solution.py:52
  15.4 45.7 %collective-permute-start.11 = (bf16[128,4416]{0,1:T(8,128)(2,1)}, bf16[128,4416]{0,1:T(8,128)(2,1)}, u32[]{:S(2)}, u32[]{:S(2)}) collective-permute-start(bf16[128,4416]{0,1:T(8,128)(2,1)} %param.23), channel_id=1, source_target_pairs={{0,2},{1,3},{2,0},{3,1},{4,6},{5,7},{6,4},{7,5},{8,10},{9,11},{10,... | collective-permute-start | bytes 3391496 | tf_op jit(solution)/shard_map/ppermute | solution.py:52
  23.1 78.5 %collective-permute-start.5 = (bf16[512,1152]{1,0:T(8,128)(2,1)}, bf16[512,1152]{1,0:T(8,128)(2,1)}, u32[]{:S(2)}, u32[]{:S(2)}) collective-permute-start(bf16[512,1152]{1,0:T(8,128)(2,1)} %copy.97), channel_id=1, source_target_pairs={{0,3},{1,2},{2,1},{3,0},{4,7},{5,6},{6,5},{7,4},{8,11},{9,10},{10,... | collective-permute-start | bytes 3538952 | tf_op jit(solution)/shard_map/ppermute | solution.py:52
  27.1 74.6 %collective-permute-start.6 = (bf16[512,1152]{1,0:T(8,128)(2,1)}, bf16[512,1152]{1,0:T(8,128)(2,1)}, u32[]{:S(2)}, u32[]{:S(2)}) collective-permute-start(bf16[512,1152]{1,0:T(8,128)(2,1)} %copy.98), channel_id=1, source_target_pairs={{0,2},{1,3},{2,0},{3,1},{4,6},{5,7},{6,4},{7,5},{8,10},{9,11},{10,... | collective-permute-start | bytes 3538952 | tf_op jit(solution)/shard_map/ppermute | solution.py:52
  35.7 12.5 %collective-permute-start.4 = (f32[2,1,640]{2,1,0:T(1,128)}, f32[2,1,640]{2,1,0:T(1,128)}, u32[]{:S(2)}, u32[]{:S(2)}) collective-permute-start(f32[2,1,640]{2,1,0:T(1,128)} %pad_maximum_fusion.15), channel_id=1, source_target_pairs={{0,1},{1,0},{2,3},{3,2},{4,5},{5,4},{6,7},{7,6},{8,9},{9,8},{10,11... | collective-permute-start | bytes 15368 | tf_op jit(solution)/shard_map/ppermute | solution.py:52
  48.1 53.6 %collective-permute-start.7 = (bf16[512,1152]{1,0:T(8,128)(2,1)}, bf16[512,1152]{1,0:T(8,128)(2,1)}, u32[]{:S(2)}, u32[]{:S(2)}) collective-permute-start(bf16[512,1152]{1,0:T(8,128)(2,1)} %copy.99), channel_id=1, source_target_pairs={{0,1},{1,0},{2,3},{3,2},{4,5},{5,4},{6,7},{7,6},{8,9},{9,8},{10,11... | collective-permute-start | bytes 3538952 | tf_op jit(solution)/shard_map/ppermute | solution.py:52
  59.4 48.1 %copy-start.4 = (bf16[512,768]{1,0:T(8,128)(2,1)}, bf16[512,768]{1,0:T(8,128)(2,1)S(1)}, u32[]{:S(2)}) copy-start(bf16[512,768]{1,0:T(8,128)(2,1)S(1)} %add_convert_fusion.5) | copy-start | bytes 2359300
  59.5 42.2 %collective-permute-start.1 = (bf16[256,768]{1,0:T(8,128)(2,1)S(1)}, bf16[256,768]{1,0:T(8,128)(2,1)S(1)}, u32[]{:S(2)}, u32[]{:S(2)}) collective-permute-start(bf16[256,768]{1,0:T(8,128)(2,1)S(1)} %constant_dynamic-slice_fusion.10), channel_id=1, source_target_pairs={{0,2},{1,3},{2,0},{3,1},{4,6},{5,7},{6,4},{7,5},{8,10},{9,11},{10,... | collective-permute-start | bytes 1179656 | tf_op jit(solution)/shard_map/ppermute | solution.py:52
  61.1 40.6 %copy-start.24 = (bf16[512,1152]{1,0:T(8,128)(2,1)S(1)}, bf16[512,1152]{1,0:T(8,128)(2,1)}, u32[]{:S(2)}) copy-start(bf16[512,1152]{1,0:T(8,128)(2,1)} %copy.100) | copy-start | bytes 3538948
  64.4 92.9 %collective-permute-start.12 = (bf16[2,128,4416]{1,2,0:T(8,128)(2,1)}, bf16[2,128,4416]{1,2,0:T(8,128)(2,1)}, u32[]{:S(2)}, u32[]{:S(2)}) collective-permute-start(bf16[2,128,4416]{1,2,0:T(8,128)(2,1)} %pad_maximum_fusion.2), channel_id=1, source_target_pairs={{0,1},{1,0},{2,3},{3,2},{4,5},{5,4},{6,7},{7,6},{8,9},{9,8},{10,11... | collective-permute-start | bytes 6782984 | tf_op jit(solution)/shard_map/ppermute | solution.py:52
  101.7 4.2 collective-permute-start.2
  125.3 9.9 %copy-start.69 = (f32[12,512]{1,0:T(8,128)}, f32[12,512]{1,0:T(8,128)S(1)}, u32[]{:S(2)}) copy-start(f32[12,512]{1,0:T(8,128)S(1)} %log_add_fusion) | copy-start | bytes 73732
  141.9 11.6 %slice-start.2 = ((s8[4718592]{0:T(1024)(128)(4,1)}), s8[4194304]{0:T(1024)(128)(4,1)S(1)}, s32[]{:S(2)}) async-start(s8[4718592]{0:T(1024)(128)(4,1)} %bitcast.546), calls=%async_computation.2 | async-start | bytes 8388608
  143.8 9.7 %copy-start.21 = (f32[512,768]{1,0:T(8,128)}, f32[512,768]{1,0:T(8,128)S(1)}, u32[]{:S(2)}) copy-start(f32[512,768]{1,0:T(8,128)S(1)} %get-tuple-element.81) | copy-start | bytes 4718596
  143.8 9.6 %copy-start.77 = (f32[512]{0:T(512)}, f32[512]{0:T(512)S(1)}, u32[]{:S(2)}) copy-start(f32[512]{0:T(512)S(1)} %broadcast_multiply_fusion.8) | copy-start | bytes 6148
  156.9 11.0 %copy-start.8 = (f32[512,768]{1,0:T(8,128)}, f32[512,768]{1,0:T(8,128)S(1)}, u32[]{:S(2)}) copy-start(f32[512,768]{1,0:T(8,128)S(1)} %get-tuple-element.79) | copy-start | bytes 4718596
  157.0 11.0 %copy-start.71 = (f32[512]{0:T(512)}, f32[512]{0:T(512)S(1)}, u32[]{:S(2)}) copy-start(f32[512]{0:T(512)S(1)} %broadcast_multiply_fusion.7) | copy-start | bytes 6148
  157.3 10.7 %copy-start.79 = (f32[512]{0:T(512)}, f32[512]{0:T(512)S(1)}, u32[]{:S(2)}) copy-start(f32[512]{0:T(512)S(1)} %add_rsqrt_fusion) | copy-start | bytes 6148
  167.6 6.2 %collective-permute-start.13 = (f32[512,69]{0,1:T(8,128)S(1)}, f32[512,69]{0,1:T(8,128)S(1)}, u32[]{:S(2)}, u32[]{:S(2)}) collective-permute-start(f32[512,69]{0,1:T(8,128)S(1)} %get-tuple-element.34), channel_id=1, source_target_pairs={{0,2},{1,3},{2,0},{3,1},{4,6},{5,7},{6,4},{7,5},{8,10},{9,11},{10,... | collective-permute-start | bytes 423944 | tf_op jit(solution)/shard_map/ppermute | solution.py:52
  174.5 13.7 %collective-permute-start.14 = (f32[2,512,69]{1,2,0:T(8,128)}, f32[2,512,69]{1,2,0:T(8,128)}, u32[]{:S(2)}, u32[]{:S(2)}) collective-permute-start(f32[2,512,69]{1,2,0:T(8,128)} %pad_maximum_fusion.7), channel_id=1, source_target_pairs={{0,1},{1,0},{2,3},{3,2},{4,5},{5,4},{6,7},{7,6},{8,9},{9,8},{10,11... | collective-permute-start | bytes 847880 | tf_op jit(solution)/shard_map/ppermute | solution.py:52
  200.3 11.2 %slice-start.6 = ((s8[4718592]{0:T(1024)(128)(4,1)}), s8[4194304]{0:T(1024)(128)(4,1)S(1)}, s32[]{:S(2)}) async-start(s8[4718592]{0:T(1024)(128)(4,1)} %bitcast.550), calls=%async_computation.6 | async-start | bytes 8388608
  299.3 80.7 %collective-permute-start.43 = (bf16[2,2,96,69]{2,3,0,1:T(8,128)(2,1)}, bf16[2,2,96,69]{2,3,0,1:T(8,128)(2,1)}, u32[]{:S(2)}, u32[]{:S(2)}) collective-permute-start(bf16[2,2,96,69]{2,3,0,1:T(8,128)(2,1)} %bitcast.487), channel_id=1, source_target_pairs={{0,4},{4,0},{8,12},{12,8},{16,20},{20,16},{24,28},{28,24},{1,5},{5... | collective-permute-start | bytes 158984 | tf_op jit(solution)/shard_map/ppermute | solution.py:57
  310.9 147.4 %collective-permute-start.38 = (bf16[2,2,384,192]{2,3,1,0:T(8,128)(2,1)}, bf16[2,2,384,192]{2,3,1,0:T(8,128)(2,1)}, u32[]{:S(2)}, u32[]{:S(2)}) collective-permute-start(bf16[2,2,384,192]{2,3,1,0:T(8,128)(2,1)} %bitcast.485), channel_id=1, source_target_pairs={{0,4},{4,0},{8,12},{12,8},{16,20},{20,16},{24,28},{28,24},{1,5},{5... | collective-permute-start | bytes 1769480 | tf_op jit(solution)/shard_map/ppermute | solution.py:57
  315.5 10.1 %copy-start.76 = (f32[512]{0:T(512)S(1)}, f32[512]{0:T(512)}, u32[]{:S(2)}) copy-start(f32[512]{0:T(512)} %copy-done.75) | copy-start | bytes 6148
  322.3 83.8 %collective-permute-start.28 = (bf16[2,2,96,192]{3,2,0,1:T(8,128)(2,1)}, bf16[2,2,96,192]{3,2,0,1:T(8,128)(2,1)}, u32[]{:S(2)}, u32[]{:S(2)}) collective-permute-start(bf16[2,2,96,192]{3,2,0,1:T(8,128)(2,1)} %bitcast.538), channel_id=1, source_target_pairs={{0,4},{4,0},{8,12},{12,8},{16,20},{20,16},{24,28},{28,24},{1,5},{5... | collective-permute-start | bytes 442376 | tf_op jit(solution)/shard_map/ppermute | solution.py:57
  353.9 45.0 %collective-permute-start.15 = (f32[136,128]{1,0:T(8,128)}, f32[136,128]{1,0:T(8,128)}, u32[]{:S(2)}, u32[]{:S(2)}) collective-permute-start(f32[136,128]{1,0:T(8,128)} %pad_bitcast_fusion), channel_id=1, source_target_pairs={{0,4},{4,0},{8,12},{12,8},{16,20},{20,16},{24,28},{28,24},{1,5},{5... | collective-permute-start | bytes 208904 | tf_op jit(solution)/shard_map/ppermute | solution.py:57
  381.6 4.0 collective-permute-start.44
  386.9 6.1 %collective-permute-start.45 = (bf16[96,69]{0,1:T(8,128)(2,1)}, bf16[96,69]{0,1:T(8,128)(2,1)}, u32[]{:S(2)}, u32[]{:S(2)}) collective-permute-start(bf16[96,69]{0,1:T(8,128)(2,1)} %dynamic-slice_bitcast_fusion.12), channel_id=1, source_target_pairs={{0,16},{4,20},{8,24},{12,28},{16,0},{20,4},{24,8},{28,12},{1,17},{... | collective-permute-start | bytes 39752 | tf_op jit(solution)/shard_map/ppermute | solution.py:57
  393.9 3.8 collective-permute-start.46
  396.4 11.2 %copy-start.62 = (bf16[2,2,1,96,192]{4,3,0,1,2:T(8,128)(2,1)S(1)}, bf16[2,2,1,96,192]{4,3,0,1,2:T(8,128)(2,1)}, u32[]{:S(2)}) copy-start(bf16[2,2,1,96,192]{4,3,0,1,2:T(8,128)(2,1)} %copy.127) | copy-start | bytes 442372
  397.3 33.8 %collective-permute-start.10 = (bf16[128,1152]{1,0:T(8,128)(2,1)}, bf16[128,1152]{1,0:T(8,128)(2,1)}, u32[]{:S(2)}, u32[]{:S(2)}) collective-permute-start(bf16[128,1152]{1,0:T(8,128)(2,1)} %get-tuple-element.113), channel_id=1, source_target_pairs={{0,1},{1,0},{2,3},{3,2},{4,5},{5,4},{6,7},{7,6},{8,9},{9,8},{10,11... | collective-permute-start | bytes 884744 | tf_op jit(solution)/shard_map/ppermute | solution.py:52
  397.7 34.1 %collective-permute-start.8 = (bf16[128,1152]{1,0:T(8,128)(2,1)}, bf16[128,1152]{1,0:T(8,128)(2,1)}, u32[]{:S(2)}, u32[]{:S(2)}) collective-permute-start(bf16[128,1152]{1,0:T(8,128)(2,1)} %get-tuple-element.114), channel_id=1, source_target_pairs={{0,3},{1,2},{2,1},{3,0},{4,7},{5,6},{6,5},{7,4},{8,11},{9,10},{10,... | collective-permute-start | bytes 884744 | tf_op jit(solution)/shard_map/ppermute | solution.py:52
  398.9 1.3 collective-permute-start.47
  400.2 4.4 collective-permute-start.16
  404.6 28.6 %collective-permute-start.9 = (bf16[128,1152]{1,0:T(8,128)(2,1)}, bf16[128,1152]{1,0:T(8,128)(2,1)}, u32[]{:S(2)}, u32[]{:S(2)}) collective-permute-start(bf16[128,1152]{1,0:T(8,128)(2,1)} %get-tuple-element.75), channel_id=1, source_target_pairs={{0,2},{1,3},{2,0},{3,1},{4,6},{5,7},{6,4},{7,5},{8,10},{9,11},{10,... | collective-permute-start | bytes 884744 | tf_op jit(solution)/shard_map/ppermute | solution.py:52
  406.1 5.3 %collective-permute-start.17 = (f32[136,128]{1,0:T(8,128)S(1)}, f32[136,128]{1,0:T(8,128)S(1)}, u32[]{:S(2)}, u32[]{:S(2)}) collective-permute-start(f32[136,128]{1,0:T(8,128)S(1)} %fusion.198), channel_id=1, source_target_pairs={{0,16},{4,20},{8,24},{12,28},{16,0},{20,4},{24,8},{28,12},{1,17},{... | collective-permute-start | bytes 208904 | tf_op jit(solution)/shard_map/ppermute | solution.py:57
  411.5 4.6 collective-permute-start.29
  416.1 5.1 collective-permute-start.30
  421.8 6.5 %collective-permute-start.31 = (bf16[96,192]{1,0:T(8,128)(2,1)}, bf16[96,192]{1,0:T(8,128)(2,1)}, u32[]{:S(2)}, u32[]{:S(2)}) collective-permute-start(bf16[96,192]{1,0:T(8,128)(2,1)} %fusion.99), channel_id=1, source_target_pairs={{0,2},{1,3},{2,0},{3,1},{4,6},{5,7},{6,4},{7,5},{8,10},{9,11},{10,... | collective-permute-start | bytes 110600 | tf_op jit(solution)/shard_map/ppermute | solution.py:52
  428.3 31.7 %collective-permute-start.33 = (bf16[2,2,96,768]{3,2,0,1:T(8,128)(2,1)}, bf16[2,2,96,768]{3,2,0,1:T(8,128)(2,1)}, u32[]{:S(2)}, u32[]{:S(2)}) collective-permute-start(bf16[2,2,96,768]{3,2,0,1:T(8,128)(2,1)} %bitcast.533), channel_id=1, source_target_pairs={{0,4},{4,0},{8,12},{12,8},{16,20},{20,16},{24,28},{28,24},{1,5},{5... | collective-permute-start | bytes 1769480 | tf_op jit(solution)/shard_map/ppermute | solution.py:57
  431.1 24.3 %collective-permute-start.23 = (bf16[2,2,96,576]{3,2,1,0:T(8,128)(2,1)}, bf16[2,2,96,576]{3,2,1,0:T(8,128)(2,1)}, u32[]{:S(2)}, u32[]{:S(2)}) collective-permute-start(bf16[2,2,96,576]{3,2,1,0:T(8,128)(2,1)} %dynamic-slice_bitcast_fusion), channel_id=1, source_target_pairs={{0,4},{4,0},{8,12},{12,8},{16,20},{20,16},{24,28},{28,24},{1,5},{5... | collective-permute-start | bytes 1327112 | tf_op jit(solution)/shard_map/ppermute | solution.py:57
  431.8 50.0 %collective-permute-start.18 = (bf16[2,2,144,768]{3,2,0,1:T(8,128)(2,1)}, bf16[2,2,144,768]{3,2,0,1:T(8,128)(2,1)}, u32[]{:S(2)}, u32[]{:S(2)}) collective-permute-start(bf16[2,2,144,768]{3,2,0,1:T(8,128)(2,1)} %bitcast.527), channel_id=1, source_target_pairs={{0,4},{4,0},{8,12},{12,8},{16,20},{20,16},{24,28},{28,24},{1,5},{5... | collective-permute-start | bytes 2654216 | tf_op jit(solution)/shard_map/ppermute | solution.py:57
  433.1 17.3 %collective-permute-start.32 = (bf16[2,96,192]{2,1,0:T(8,128)(2,1)}, bf16[2,96,192]{2,1,0:T(8,128)(2,1)}, u32[]{:S(2)}, u32[]{:S(2)}) collective-permute-start(bf16[2,96,192]{2,1,0:T(8,128)(2,1)} %pad_maximum_fusion.11), channel_id=1, source_target_pairs={{0,1},{1,0},{2,3},{3,2},{4,5},{5,4},{6,7},{7,6},{8,9},{9,8},{10,11... | collective-permute-start | bytes 221192 | tf_op jit(solution)/shard_map/ppermute | solution.py:52
  456.6 10.3 %collective-permute-start.24 = (bf16[2,96,576]{2,1,0:T(8,128)(2,1)S(1)}, bf16[2,96,576]{2,1,0:T(8,128)(2,1)S(1)}, u32[]{:S(2)}, u32[]{:S(2)}) collective-permute-start(bf16[2,96,576]{2,1,0:T(8,128)(2,1)S(1)} %dynamic-slice_bitcast_fusion.4), channel_id=1, source_target_pairs={{0,8},{4,12},{8,0},{12,4},{16,24},{20,28},{24,16},{28,20},{1,9},{5... | collective-permute-start | bytes 663560 | tf_op jit(solution)/shard_map/ppermute | solution.py:57
  459.5 16.6 %collective-permute-start.39 = (bf16[2,384,192]{1,2,0:T(8,128)(2,1)S(1)}, bf16[2,384,192]{1,2,0:T(8,128)(2,1)S(1)}, u32[]{:S(2)}, u32[]{:S(2)}) collective-permute-start(bf16[2,384,192]{1,2,0:T(8,128)(2,1)S(1)} %dynamic-slice_bitcast_fusion.2), channel_id=1, source_target_pairs={{0,8},{4,12},{8,0},{12,4},{16,24},{20,28},{24,16},{28,20},{1,9},{5... | collective-permute-start | bytes 884744 | tf_op jit(solution)/shard_map/ppermute | solution.py:57
  467.0 14.8 %copy-start.47 = (bf16[2,2,1,144,768]{4,3,2,1,0:T(8,128)(2,1)S(1)}, bf16[2,2,1,144,768]{4,3,2,1,0:T(8,128)(2,1)}, u32[]{:S(2)}) copy-start(bf16[2,2,1,144,768]{4,3,2,1,0:T(8,128)(2,1)} %get-tuple-element.101) | copy-start | bytes 2654212
  467.0 8.0 %collective-permute-start.25 = (bf16[96,576]{1,0:T(8,128)(2,1)S(1)}, bf16[96,576]{1,0:T(8,128)(2,1)S(1)}, u32[]{:S(2)}, u32[]{:S(2)}) collective-permute-start(bf16[96,576]{1,0:T(8,128)(2,1)S(1)} %dynamic-slice_bitcast_fusion.8), channel_id=1, source_target_pairs={{0,16},{4,20},{8,24},{12,28},{16,0},{20,4},{24,8},{28,12},{1,17},{... | collective-permute-start | bytes 331784 | tf_op jit(solution)/shard_map/ppermute | solution.py:57
  468.1 11.3 %collective-permute-start.34 = (bf16[2,96,768]{2,1,0:T(8,128)(2,1)S(1)}, bf16[2,96,768]{2,1,0:T(8,128)(2,1)S(1)}, u32[]{:S(2)}, u32[]{:S(2)}) collective-permute-start(bf16[2,96,768]{2,1,0:T(8,128)(2,1)S(1)} %dynamic-slice_bitcast_fusion.3), channel_id=1, source_target_pairs={{0,8},{4,12},{8,0},{12,4},{16,24},{20,28},{24,16},{28,20},{1,9},{5... | collective-permute-start | bytes 884744 | tf_op jit(solution)/shard_map/ppermute | solution.py:57
  475.1 9.6 %collective-permute-start.26 = (bf16[96,576]{1,0:T(8,128)(2,1)S(1)}, bf16[96,576]{1,0:T(8,128)(2,1)S(1)}, u32[]{:S(2)}, u32[]{:S(2)}) collective-permute-start(bf16[96,576]{1,0:T(8,128)(2,1)S(1)} %fusion.86), channel_id=1, source_target_pairs={{0,2},{1,3},{2,0},{3,1},{4,6},{5,7},{6,4},{7,5},{8,10},{9,11},{10,... | collective-permute-start | bytes 331784 | tf_op jit(solution)/shard_map/ppermute | solution.py:52
  476.2 8.8 %collective-permute-start.40 = (bf16[384,192]{0,1:T(8,128)(2,1)S(1)}, bf16[384,192]{0,1:T(8,128)(2,1)S(1)}, u32[]{:S(2)}, u32[]{:S(2)}) collective-permute-start(bf16[384,192]{0,1:T(8,128)(2,1)S(1)} %dynamic-slice_bitcast_fusion.6), channel_id=1, source_target_pairs={{0,16},{4,20},{8,24},{12,28},{16,0},{20,4},{24,8},{28,12},{1,17},{... | collective-permute-start | bytes 442376 | tf_op jit(solution)/shard_map/ppermute | solution.py:57
  479.5 8.0 %collective-permute-start.35 = (bf16[96,768]{1,0:T(8,128)(2,1)S(1)}, bf16[96,768]{1,0:T(8,128)(2,1)S(1)}, u32[]{:S(2)}, u32[]{:S(2)}) collective-permute-start(bf16[96,768]{1,0:T(8,128)(2,1)S(1)} %dynamic-slice_bitcast_fusion.7), channel_id=1, source_target_pairs={{0,16},{4,20},{8,24},{12,28},{16,0},{20,4},{24,8},{28,12},{1,17},{... | collective-permute-start | bytes 442376 | tf_op jit(solution)/shard_map/ppermute | solution.py:57
  484.1 12.2 %collective-permute-start.19 = (bf16[2,144,768]{2,1,0:T(8,128)(2,1)}, bf16[2,144,768]{2,1,0:T(8,128)(2,1)}, u32[]{:S(2)}, u32[]{:S(2)}) collective-permute-start(bf16[2,144,768]{2,1,0:T(8,128)(2,1)} %dynamic-slice_bitcast_fusion.1), channel_id=1, source_target_pairs={{0,8},{4,12},{8,0},{12,4},{16,24},{20,28},{24,16},{28,20},{1,9},{5... | collective-permute-start | bytes 1327112 | tf_op jit(solution)/shard_map/ppermute | solution.py:57
  484.7 3.8 collective-permute-start.27
  485.7 7.7 %collective-permute-start.41 = (bf16[384,192]{0,1:T(8,128)(2,1)}, bf16[384,192]{0,1:T(8,128)(2,1)}, u32[]{:S(2)}, u32[]{:S(2)}) collective-permute-start(bf16[384,192]{0,1:T(8,128)(2,1)} %fusion.82), channel_id=1, source_target_pairs={{0,2},{1,3},{2,0},{3,1},{4,6},{5,7},{6,4},{7,5},{8,10},{9,11},{10,... | collective-permute-start | bytes 442376 | tf_op jit(solution)/shard_map/ppermute | solution.py:52
  488.2 7.1 %collective-permute-start.36 = (bf16[96,768]{1,0:T(8,128)(2,1)}, bf16[96,768]{1,0:T(8,128)(2,1)}, u32[]{:S(2)}, u32[]{:S(2)}) collective-permute-start(bf16[96,768]{1,0:T(8,128)(2,1)} %fusion.83), channel_id=1, source_target_pairs={{0,2},{1,3},{2,0},{3,1},{4,6},{5,7},{6,4},{7,5},{8,10},{9,11},{10,... | collective-permute-start | bytes 442376 | tf_op jit(solution)/shard_map/ppermute | solution.py:52
  494.4 5.8 %collective-permute-start.42 = (bf16[2,384,192]{1,2,0:T(8,128)(2,1)S(1)}, bf16[2,384,192]{1,2,0:T(8,128)(2,1)S(1)}, u32[]{:S(2)}, u32[]{:S(2)}) collective-permute-start(bf16[2,384,192]{1,2,0:T(8,128)(2,1)S(1)} %pad_maximum_fusion.9), channel_id=1, source_target_pairs={{0,1},{1,0},{2,3},{3,2},{4,5},{5,4},{6,7},{7,6},{8,9},{9,8},{10,11... | collective-permute-start | bytes 884744 | tf_op jit(solution)/shard_map/ppermute | solution.py:52
  496.2 16.4 %collective-permute-start.37 = (bf16[2,96,768]{2,1,0:T(8,128)(2,1)S(1)}, bf16[2,96,768]{2,1,0:T(8,128)(2,1)S(1)}, u32[]{:S(2)}, u32[]{:S(2)}) collective-permute-start(bf16[2,96,768]{2,1,0:T(8,128)(2,1)S(1)} %pad_maximum_fusion.8), channel_id=1, source_target_pairs={{0,1},{1,0},{2,3},{3,2},{4,5},{5,4},{6,7},{7,6},{8,9},{9,8},{10,11... | collective-permute-start | bytes 884744 | tf_op jit(solution)/shard_map/ppermute | solution.py:52
  497.5 13.5 %collective-permute-start.20 = (bf16[144,768]{1,0:T(8,128)(2,1)S(1)}, bf16[144,768]{1,0:T(8,128)(2,1)S(1)}, u32[]{:S(2)}, u32[]{:S(2)}) collective-permute-start(bf16[144,768]{1,0:T(8,128)(2,1)S(1)} %dynamic-slice_bitcast_fusion.5), channel_id=1, source_target_pairs={{0,16},{4,20},{8,24},{12,28},{16,0},{20,4},{24,8},{28,12},{1,17},{... | collective-permute-start | bytes 663560 | tf_op jit(solution)/shard_map/ppermute | solution.py:57
  511.1 7.1 %collective-permute-start.21 = (bf16[144,768]{1,0:T(8,128)(2,1)S(1)}, bf16[144,768]{1,0:T(8,128)(2,1)S(1)}, u32[]{:S(2)}, u32[]{:S(2)}) collective-permute-start(bf16[144,768]{1,0:T(8,128)(2,1)S(1)} %fusion.69), channel_id=1, source_target_pairs={{0,2},{1,3},{2,0},{3,1},{4,6},{5,7},{6,4},{7,5},{8,10},{9,11},{10,... | collective-permute-start | bytes 663560 | tf_op jit(solution)/shard_map/ppermute | solution.py:52
  519.0 6.0 %collective-permute-start.22 = (bf16[2,144,768]{2,1,0:T(8,128)(2,1)}, bf16[2,144,768]{2,1,0:T(8,128)(2,1)}, u32[]{:S(2)}, u32[]{:S(2)}) collective-permute-start(bf16[2,144,768]{2,1,0:T(8,128)(2,1)} %pad_maximum_fusion.6), channel_id=1, source_target_pairs={{0,1},{1,0},{2,3},{3,2},{4,5},{5,4},{6,7},{7,6},{8,9},{9,8},{10,11... | collective-permute-start | bytes 1327112 | tf_op jit(solution)/shard_map/ppermute | solution.py:52
  (111 other events, 439.3 us)
